TPU v7x, 128 devices: a whole 4x4x4 slice. The times are simulated.
128 devices in a mesh: section: 4 (over y_lo, core), dp: 4 (over z), node: 8 (over y_hi, x).
Axes of the slice: x: 4, y: 4 (y_hi: 2, y_lo: 2; y = y_hi * 2 + y_lo), z: 4, core: 2. Of those that a mesh axis runs over, the one named last changes fastest.
Arguments:
- grad_out: bfloat16 [2, 256, 3072], P(None, ('dp', 'node')), may hold values from -6 to 6
- layer_in: bfloat16 [4, 2, 256, 3072], P('section', None, ('dp', 'node')), may hold values from -6 to 6
- gate_pre: bfloat16 [4, 2, 256, 8192], P('section', None, 'dp', 'node'), may hold values from -6 to 6
- up_pre: bfloat16 [4, 2, 256, 8192], P('section', None, 'dp', 'node'), may hold values from -6 to 6
- expert_ids: int32 [4, 2, 256, 2], P('section', None, 'dp'), may hold values from 0 to 7, as said below
- route_weight: float32 [4, 2, 256, 2], P('section', None, 'dp'), may hold values from 0.3 to 1
- w_gate: bfloat16 [4, 3072, 8192], P('section', None, 'node'), may hold values from -0.109375 to 0.109375
- w_up: bfloat16 [4, 3072, 8192], P('section', None, 'node'), may hold values from -0.109375 to 0.109375
- w_down: bfloat16 [4, 8192, 3072], P('section', 'node'), may hold values from -0.0625 to 0.0625
Outputs:
- grad_in: bfloat16 [4, 2, 256, 3072], P('section', None, ('dp', 'node'))
- grad_gate_w: bfloat16 [4, 3072, 8192], P('section', 'dp', 'node')
- grad_up_w: bfloat16 [4, 3072, 8192], P('section', 'dp', 'node')
- grad_down_w: bfloat16 [4, 8192, 3072], P('section', 'node', 'dp')
Inputs may be any that keep to these rules, and one draw needn't show every extreme that they name: `expert_ids`: each token names 2 different experts.
All inputs are finite; a program needn't handle non-finite values.
Results may differ from a plain program's by a relative error of at most 0.025.
Values may be sent and summed in bfloat16 or wider, within the bound.
A program may use at most 192 MiB of HBM per device.

v0:
```python
import jax
import jax.numpy as jnp
from jax import lax
from jax.sharding import PartitionSpec as P


def passed_along(value, axis, steps):
    count = lax.axis_size(axis)
    leading, last = (max(0, -steps), min(count, count - steps))
    return lax.ppermute(value, axis, [(source, source + steps) for source in range(leading, last)])


def shards(grad_out, layer_in, gate_pre, up_pre, expert_ids, route_weight, w_gate, w_up, w_down):
    sections = lax.axis_size("section")
    position = lax.axis_index("section")
    micro = grad_out.shape[0]
    rows = grad_out.shape[1]
    width = grad_out.shape[2]
    gate_w = w_gate[0]
    up_w = w_up[0]
    down_w = w_down[0]
    carry = jnp.zeros((rows, width), jnp.bfloat16)
    acc_gate = jnp.zeros(gate_w.shape, jnp.float32)
    acc_up = jnp.zeros(up_w.shape, jnp.float32)
    acc_down = jnp.zeros(down_w.shape, jnp.float32)
    outputs = jnp.zeros((micro, rows, width), jnp.bfloat16)
    is_last = position == sections - 1
    for moment in range(sections + micro - 1):
        batch = moment - (sections - 1) + position
        valid = jnp.logical_and(batch >= 0, batch < micro)
        pick = jnp.clip(batch, 0, micro - 1)
        incoming = passed_along(carry, "section", -1)
        grad_now = jnp.where(
            is_last, lax.dynamic_index_in_dim(grad_out, pick, 0, keepdims=False), incoming
        )
        grad_all = lax.all_gather(grad_now, "node", axis=0, tiled=True)
        inputs_now = lax.all_gather(
            lax.dynamic_index_in_dim(layer_in[0], pick, 0, keepdims=False),
            "node",
            axis=0,
            tiled=True,
        )
        gate = lax.dynamic_index_in_dim(gate_pre[0], pick, 0, keepdims=False).astype(jnp.float32)
        upval = lax.dynamic_index_in_dim(up_pre[0], pick, 0, keepdims=False).astype(jnp.float32)
        named = lax.dynamic_index_in_dim(expert_ids[0], pick, 0, keepdims=False)
        weights = lax.dynamic_index_in_dim(route_weight[0], pick, 0, keepdims=False)
        coef = jnp.sum(jnp.where(named == 0, weights, jnp.float32(0.0)), axis=-1)[:, None]
        back = (
            lax.dot_general(
                grad_all, down_w, (((1,), (1,)), ((), ())), preferred_element_type=jnp.float32
            )
            * coef
        )
        sigma = jax.nn.sigmoid(gate)
        active = gate * sigma
        d_gate = (back * upval * sigma * (1.0 + gate * (1.0 - sigma))).astype(jnp.bfloat16)
        d_up = (back * active).astype(jnp.bfloat16)
        hidden = (coef * active * upval).astype(jnp.bfloat16)
        keep = valid.astype(jnp.float32)
        acc_gate = acc_gate + keep * lax.dot_general(
            inputs_now, d_gate, (((0,), (0,)), ((), ())), preferred_element_type=jnp.float32
        )
        acc_up = acc_up + keep * lax.dot_general(
            inputs_now, d_up, (((0,), (0,)), ((), ())), preferred_element_type=jnp.float32
        )
        acc_down = acc_down + keep * lax.dot_general(
            hidden, grad_all, (((0,), (0,)), ((), ())), preferred_element_type=jnp.float32
        )
        first_term = lax.dot_general(
            d_gate, gate_w, (((1,), (1,)), ((), ())), preferred_element_type=jnp.float32
        )
        summed = lax.psum_scatter(
            (
                first_term
                + lax.dot_general(
                    d_up, up_w, (((1,), (1,)), ((), ())), preferred_element_type=jnp.float32
                )
            ).astype(jnp.bfloat16),
            "node",
            scatter_dimension=0,
            tiled=True,
        ).astype(jnp.float32)
        result = (grad_now.astype(jnp.float32) + summed).astype(jnp.bfloat16)
        outputs = jnp.where(
            valid, lax.dynamic_update_index_in_dim(outputs, result, pick, 0), outputs
        )
        carry = result
    grad_gate, grad_up = (
        lax.psum_scatter(
            acc_gate.astype(jnp.bfloat16), "dp", scatter_dimension=0, tiled=True
        ).astype(jnp.float32),
        lax.psum_scatter(acc_up.astype(jnp.bfloat16), "dp", scatter_dimension=0, tiled=True).astype(
            jnp.float32
        ),
    )
    grad_down = lax.psum_scatter(
        acc_down.astype(jnp.bfloat16), "dp", scatter_dimension=1, tiled=True
    )
    return (
        outputs[None],
        grad_gate.astype(jnp.bfloat16)[None],
        grad_up.astype(jnp.bfloat16)[None],
        grad_down[None],
    )


def solution(mesh):
    return jax.shard_map(
        shards,
        mesh=mesh,
        in_specs=(
            P(None, ("dp", "node"), None),
            P("section", None, ("dp", "node"), None),
            P("section", None, "dp", "node"),
            P("section", None, "dp", "node"),
            P("section", None, "dp", None),
            P("section", None, "dp", None),
            P("section", None, "node"),
            P("section", None, "node"),
            P("section", "node", None),
        ),
        out_specs=(
            P("section", None, ("dp", "node"), None),
            P("section", "dp", "node"),
            P("section", "dp", "node"),
            P("section", "node", "dp"),
        ),
        check_vma=False,
    )
```

profile of v0, /device:TPU:0, one launch (start us, length us, event | category | flops | bytes accessed | tf_op | source)
XLA Modules:
  0.0 947.9 jit_solution(8852921775724777233)
XLA Ops:
  11.3 35.3 %all_gather.30 = bf16[64,3072]{1,0:T(8,128)(2,1)S(1)} all-gather(bf16[8,3072]{1,0:T(8,128)(2,1)S(1)} %bitcast_select_fusion.7), channel_id=1, replica_groups=mesh['section'=4,'dp'=4,'node'=8] {'node'}, dimensions={0}, use_global_device_ids=true | all-gather | bytes 442368 | tf_op jit(solution)/shard_map/all_gather | solution.py:36
  47.4 5.1 fusion.95
  53.1 4.8 fusion.8
  57.9 2.8 fusion.57
  60.8 73.2 %reduce-scatter.9.cloned.1.call-done = bf16[8,3072]{1,0:T(8,128)(2,1)} async-done(((bf16[64,3072]{1,0:T(8,128)(2,1)}), bf16[8,3072]{1,0:T(8,128)(2,1)}) %reduce-scatter.9.cloned.1.call-update) | async-done | bytes 49168 | tf_op jit(solution)/shard_map/reduce_scatter | solution.py:72
  136.2 1.8 collective-permute-done.1
  138.0 34.6 %all_gather.31 = bf16[64,3072]{1,0:T(8,128)(2,1)S(1)} all-gather(bf16[8,3072]{1,0:T(8,128)(2,1)S(1)} %bitcast_select_fusion.6), channel_id=1, replica_groups=mesh['section'=4,'dp'=4,'node'=8] {'node'}, dimensions={0}, use_global_device_ids=true | all-gather | bytes 442368 | tf_op jit(solution)/shard_map/all_gather | solution.py:36
  173.4 4.8 fusion.99
  178.3 4.9 fusion.6
  183.2 5.6 fusion.54
  188.8 70.4 %reduce-scatter.11.cloned.1.call-done = bf16[8,3072]{1,0:T(8,128)(2,1)} async-done(((bf16[64,3072]{1,0:T(8,128)(2,1)}), bf16[8,3072]{1,0:T(8,128)(2,1)}) %reduce-scatter.11.cloned.1.call-update) | async-done | bytes 49168 | tf_op jit(solution)/shard_map/reduce_scatter | solution.py:72
  263.2 34.8 %all_gather.32 = bf16[64,3072]{1,0:T(8,128)(2,1)S(1)} all-gather(bf16[8,3072]{1,0:T(8,128)(2,1)S(1)} %bitcast_select_fusion.4), channel_id=1, replica_groups=mesh['section'=4,'dp'=4,'node'=8] {'node'}, dimensions={0}, use_global_device_ids=true | all-gather | bytes 442368 | tf_op jit(solution)/shard_map/all_gather | solution.py:36
  298.0 5.0 fusion.103
  303.0 4.9 fusion.4
  308.0 5.7 fusion.51
  313.8 35.0 %all-gather.3 = bf16[1,1,64,3072]{3,2,1,0:T(8,128)(2,1)S(1)} all-gather(bf16[1,1,8,3072]{3,2,1,0:T(8,128)(2,1)S(1)} %get-tuple-element.31), channel_id=5, replica_groups=mesh['section'=4,'dp'=4,'node'=8] {'node'}, dimensions={2}, use_global_device_ids=true | all-gather | bytes 442368 | tf_op jit(solution)/shard_map/all_gather | solution.py:37
  348.7 34.9 %all-gather.2 = bf16[1,1,64,3072]{3,2,1,0:T(8,128)(2,1)S(1)} all-gather(bf16[1,1,8,3072]{3,2,1,0:T(8,128)(2,1)} %get-tuple-element.28), channel_id=4, replica_groups=mesh['section'=4,'dp'=4,'node'=8] {'node'}, dimensions={2}, use_global_device_ids=true | all-gather | bytes 442368 | tf_op jit(solution)/shard_map/all_gather | solution.py:37
  383.6 36.8 %all-gather.1 = bf16[1,1,64,3072]{3,2,1,0:T(8,128)(2,1)} all-gather(bf16[1,1,8,3072]{3,2,1,0:T(8,128)(2,1)} %get-tuple-element.29), channel_id=3, replica_groups=mesh['section'=4,'dp'=4,'node'=8] {'node'}, dimensions={2}, use_global_device_ids=true | all-gather | bytes 442368 | tf_op jit(solution)/shard_map/all_gather | solution.py:37
  420.5 36.8 %all-gather = bf16[1,1,64,3072]{3,2,1,0:T(8,128)(2,1)} all-gather(bf16[1,1,8,3072]{3,2,1,0:T(8,128)(2,1)} %get-tuple-element.30), channel_id=2, replica_groups=mesh['section'=4,'dp'=4,'node'=8] {'node'}, dimensions={2}, use_global_device_ids=true | all-gather | bytes 442368 | tf_op jit(solution)/shard_map/all_gather | solution.py:37
  457.3 36.8 %all-gather.4 = bf16[1,1,64,3072]{3,2,1,0:T(8,128)(2,1)} all-gather(bf16[1,1,8,3072]{3,2,1,0:T(8,128)(2,1)} %get-tuple-element.27), channel_id=6, replica_groups=mesh['section'=4,'dp'=4,'node'=8] {'node'}, dimensions={2}, use_global_device_ids=true | all-gather | bytes 442368 | tf_op jit(solution)/shard_map/all_gather | solution.py:37
  495.0 1.6 collective-permute-start.3
  496.6 8.1 fusion.91
  504.8 34.8 %all_gather.33 = bf16[64,3072]{1,0:T(8,128)(2,1)S(1)} all-gather(bf16[8,3072]{1,0:T(8,128)(2,1)S(1)} %bitcast_select_fusion.2), channel_id=1, replica_groups=mesh['section'=4,'dp'=4,'node'=8] {'node'}, dimensions={0}, use_global_device_ids=true | all-gather | bytes 442368 | tf_op jit(solution)/shard_map/all_gather | solution.py:36
  539.6 2.1 fusion.107
  541.7 2.0 fusion.2
  543.8 2.8 fusion.48
  546.8 7.4 fusion.87
  554.3 6.4 fusion.83
  560.7 57.5 %reduce-scatter.15.cloned.1.call-done = bf16[8,3072]{1,0:T(8,128)(2,1)} async-done(((bf16[64,3072]{1,0:T(8,128)(2,1)}), bf16[8,3072]{1,0:T(8,128)(2,1)}) %reduce-scatter.15.cloned.1.call-update) | async-done | bytes 49168 | tf_op jit(solution)/shard_map/reduce_scatter | solution.py:72
  620.6 8.0 fusion.79
  628.6 34.8 %all_gather.34 = bf16[64,3072]{1,0:T(8,128)(2,1)S(1)} all-gather(bf16[8,3072]{1,0:T(8,128)(2,1)S(1)} %bitcast_select_fusion), channel_id=1, replica_groups=mesh['section'=4,'dp'=4,'node'=8] {'node'}, dimensions={0}, use_global_device_ids=true | all-gather | bytes 442368 | tf_op jit(solution)/shard_map/all_gather | solution.py:36
  663.5 2.1 fusion.111
  665.6 2.0 fusion
  667.7 2.8 fusion.45
  670.5 20.2 %add_convert_fusion.2 = bf16[3072,1024]{1,0:T(8,128)(2,1)} fusion(f32[3072,1024]{1,0:T(8,128)} %fusion.79, f32[3072,1024]{1,0:T(8,128)} %fusion.83, f32[3072,1024]{1,0:T(8,128)} %fusion.87, f32[3072,1024]{1,0:T(8,128)} %fusion.91, bf16[64,1024]{1,0:T(8,128)(2,1)} %copy-done.28, f32[]{:T(128)S(6)} %convert_element_type.247, f32[]{:T(128)S(6)} %convert_element_type.246, ...), kind=kOutput, calls=%fused_computation.2 | convolution fusion | flops 434110464 | bytes 57147412 | tf_op jit(solution)/shard_map/dot_general | solution.py:60
  691.2 2.8 fusion.89
  694.1 7.3 fusion.85
  701.4 6.4 fusion.81
  707.8 6.4 fusion.77
  714.3 16.7 %add_convert_fusion.1 = bf16[3072,1024]{1,0:T(8,128)(2,1)} fusion(f32[3072,1024]{1,0:T(8,128)} %fusion.77, f32[3072,1024]{1,0:T(8,128)} %fusion.81, f32[3072,1024]{1,0:T(8,128)} %fusion.85, f32[3072,1024]{1,0:T(8,128)S(1)} %fusion.89, bf16[64,1024]{1,0:T(8,128)(2,1)S(1)} %copy-done.22, f32[]{:T(128)S(6)} %convert_element_type.247, ...), kind=kOutput, calls=%fused_computation.1 | convolution fusion | flops 434110464 | bytes 57147412 | tf_op jit(solution)/shard_map/dot_general | solution.py:63
  731.3 1.9 fusion.140
  733.2 6.5 fusion.138
  739.7 6.5 fusion.136
  746.2 7.2 fusion.134
  753.5 17.1 %add_convert_fusion = bf16[1024,3072]{1,0:T(8,128)(2,1)} fusion(f32[1024,3072]{1,0:T(8,128)} %fusion.134, f32[1024,3072]{1,0:T(8,128)} %fusion.136, f32[1024,3072]{1,0:T(8,128)} %fusion.138, f32[1024,3072]{1,0:T(8,128)S(1)} %fusion.140, bf16[64,3072]{1,0:T(8,128)(2,1)S(1)} %copy-done.5, f32[]{:T(128)S(6)} %convert_element_type.247, ...), kind=kOutput, calls=%fused_computation | convolution fusion | flops 434700288 | bytes 57279000 | tf_op jit(solution)/shard_map/dot_general | solution.py:66
  771.4 35.9 %reduce-scatter.19.cloned.1.call-done = bf16[768,1024]{1,0:T(8,128)(2,1)} async-done(((bf16[3072,1024]{1,0:T(8,128)(2,1)}), bf16[768,1024]{1,0:T(8,128)(2,1)}) %reduce-scatter.19.cloned.1.call-update) | async-done | bytes 1572880 | tf_op jit(solution)/shard_map/reduce_scatter | solution.py:89
  807.3 66.7 %reduce-scatter.21.cloned.1.call-done = bf16[768,1024]{1,0:T(8,128)(2,1)} async-done(((bf16[3072,1024]{1,0:T(8,128)(2,1)}), bf16[768,1024]{1,0:T(8,128)(2,1)}) %reduce-scatter.21.cloned.1.call-update) | async-done | bytes 1572880 | tf_op jit(solution)/shard_map/reduce_scatter | solution.py:92
  874.1 66.7 %reduce-scatter.23.cloned.1.call-done = bf16[1024,768]{1,0:T(8,128)(2,1)} async-done(((bf16[1024,3072]{1,0:T(8,128)(2,1)}), bf16[1024,768]{1,0:T(8,128)(2,1)}) %reduce-scatter.23.cloned.1.call-update) | async-done | bytes 1572880 | tf_op jit(solution)/shard_map/reduce_scatter | solution.py:96
  (164 shorter events, 17.9 us)
Async XLA Ops:
  7.2 130.8 %copy-start.30 = (bf16[2,8,3072]{2,1,0:T(8,128)(2,1)S(1)}, bf16[2,8,3072]{2,1,0:T(8,128)(2,1)}, u32[]{:S(2)}) copy-start(bf16[2,8,3072]{2,1,0:T(8,128)(2,1)} %param.9) | copy-start | bytes 294916
  7.2 166.2 %copy-start = (bf16[1,2,64,1024]{3,2,1,0:T(8,128)(2,1)S(1)}, bf16[1,2,64,1024]{3,2,1,0:T(8,128)(2,1)}, u32[]{:S(2)}) copy-start(bf16[1,2,64,1024]{3,2,1,0:T(8,128)(2,1)} %param.11) | copy-start | bytes 786436
  7.2 166.2 %copy-start.1 = (bf16[1,2,64,1024]{3,2,1,0:T(8,128)(2,1)S(1)}, bf16[1,2,64,1024]{3,2,1,0:T(8,128)(2,1)}, u32[]{:S(2)}) copy-start(bf16[1,2,64,1024]{3,2,1,0:T(8,128)(2,1)} %param.12) | copy-start | bytes 786436
  7.2 50.7 %slice-start.8 = ((s8[6291456]{0:T(1024)(128)(4,1)}), s8[2097152]{0:T(1024)(128)(4,1)S(1)}, s32[]{:S(2)}) async-start(s8[6291456]{0:T(1024)(128)(4,1)} %bitcast.256), calls=%async_computation.24 | async-start | bytes 4194304
  7.2 126.8 %reduce-scatter.9.cloned.1.call-start = ((), (), s32[]{:S(2)}) async-start(), calls=%async_computation.8 | async-start | bytes 442368 | tf_op jit(solution)/shard_map/reduce_scatter | solution.py:72
  7.3 3.3 collective-permute-start
  10.3 125.9 %copy-start.40 = (f32[64]{0:T(128)}, f32[64]{0:T(128)S(1)}, u32[]{:S(2)}) copy-start(f32[64]{0:T(128)S(1)} %get-tuple-element.7) | copy-start | bytes 772
  10.3 168.0 %copy-start.38 = (f32[64]{0:T(128)}, f32[64]{0:T(128)S(1)}, u32[]{:S(2)}) copy-start(f32[64]{0:T(128)S(1)} %get-tuple-element.6) | copy-start | bytes 772
  10.3 287.7 %copy-start.36 = (f32[64]{0:T(128)}, f32[64]{0:T(128)S(1)}, u32[]{:S(2)}) copy-start(f32[64]{0:T(128)S(1)} %get-tuple-element.5) | copy-start | bytes 772
  47.4 10.5 %slice-start.9 = ((s8[6291456]{0:T(1024)(128)(4,1)}), s8[4194304]{0:T(1024)(128)(4,1)S(1)}, s32[]{:S(2)}) async-start(s8[6291456]{0:T(1024)(128)(4,1)} %bitcast.256), calls=%async_computation.25 | async-start | bytes 8388608
  60.7 200.7 %copy-start.29 = (bf16[1,2,8,3072]{3,2,1,0:T(8,128)(2,1)S(1)}, bf16[1,2,8,3072]{3,2,1,0:T(8,128)(2,1)}, u32[]{:S(2)}) copy-start(bf16[1,2,8,3072]{3,2,1,0:T(8,128)(2,1)} %param.10) | copy-start | bytes 294916
  60.7 198.5 %reduce-scatter.11.cloned.1.call-start = ((), (), s32[]{:S(2)}) async-start(), calls=%async_computation.9 | async-start | bytes 442368 | tf_op jit(solution)/shard_map/reduce_scatter | solution.py:72
  134.9 3.1 collective-permute-start.1
  178.2 119.7 %copy-start.24 = (bf16[64,1024]{1,0:T(8,128)(2,1)}, bf16[64,1024]{1,0:T(8,128)(2,1)S(1)}, u32[]{:S(2)}) copy-start(bf16[64,1024]{1,0:T(8,128)(2,1)S(1)} %get-tuple-element.23) | copy-start | bytes 393220
  178.3 129.7 %copy-start.16 = (bf16[64,1024]{1,0:T(8,128)(2,1)}, bf16[64,1024]{1,0:T(8,128)(2,1)S(1)}, u32[]{:S(2)}) copy-start(bf16[64,1024]{1,0:T(8,128)(2,1)S(1)} %get-tuple-element.24) | copy-start | bytes 393220
  188.8 305.4 %reduce-scatter.13.cloned.1.call-start = ((), (), s32[]{:S(2)}) async-start(), calls=%async_computation.10 | async-start | bytes 442368 | tf_op jit(solution)/shard_map/reduce_scatter | solution.py:72
  260.1 3.1 collective-permute-start.2
  303.0 10.7 %copy-start.17 = (bf16[64,1024]{1,0:T(8,128)(2,1)}, bf16[64,1024]{1,0:T(8,128)(2,1)S(1)}, u32[]{:S(2)}) copy-start(bf16[64,1024]{1,0:T(8,128)(2,1)S(1)} %get-tuple-element.22) | copy-start | bytes 393220
  303.0 10.7 %copy-start.25 = (bf16[64,1024]{1,0:T(8,128)(2,1)}, bf16[64,1024]{1,0:T(8,128)(2,1)S(1)}, u32[]{:S(2)}) copy-start(bf16[64,1024]{1,0:T(8,128)(2,1)S(1)} %get-tuple-element.21) | copy-start | bytes 393220
  307.9 231.6 %slice-start.4 = ((s8[6291456]{0:T(1024)(128)(4,1)}), s8[2097152]{0:T(1024)(128)(4,1)S(1)}, s32[]{:S(2)}) async-start(s8[6291456]{0:T(1024)(128)(4,1)} %bitcast.252), calls=%async_computation.20 | async-start | bytes 4194304
  313.7 304.5 %reduce-scatter.15.cloned.1.call-start = ((), (), s32[]{:S(2)}) async-start(), calls=%async_computation.11 | async-start | bytes 442368 | tf_op jit(solution)/shard_map/reduce_scatter | solution.py:72
  494.1 10.6 %copy-start.31 = (bf16[2,8,3072]{2,1,0:T(8,128)(2,1)S(1)}, bf16[2,8,3072]{2,1,0:T(8,128)(2,1)}, u32[]{:S(2)}) copy-start(bf16[2,8,3072]{2,1,0:T(8,128)(2,1)} %param.9) | copy-start | bytes 294916
  494.1 45.4 %copy-start.34 = (f32[64]{0:T(128)S(1)}, f32[64]{0:T(128)}, u32[]{:S(2)}) copy-start(f32[64]{0:T(128)} %get-tuple-element.8) | copy-start | bytes 772
  495.0 46.7 %slice-start = ((s8[6291456]{0:T(1024)(128)(4,1)}), s8[4194304]{0:T(1024)(128)(4,1)S(1)}, s32[]{:S(2)}) async-start(s8[6291456]{0:T(1024)(128)(4,1)} %bitcast.248), calls=%async_computation.16 | async-start | bytes 8388608
  495.0 44.5 %slice-start.5 = ((s8[6291456]{0:T(1024)(128)(4,1)}), s8[4194304]{0:T(1024)(128)(4,1)S(1)}, s32[]{:S(2)}) async-start(s8[6291456]{0:T(1024)(128)(4,1)} %bitcast.252), calls=%async_computation.21 | async-start | bytes 8388608
  495.0 46.7 %slice-start.1 = ((s8[6291456]{0:T(1024)(128)(4,1)}), s8[2097152]{0:T(1024)(128)(4,1)S(1)}, s32[]{:S(2)}) async-start(s8[6291456]{0:T(1024)(128)(4,1)} %bitcast.248), calls=%async_computation.17 | async-start | bytes 4194304
  495.0 9.7 %collective-permute-start.3 = (bf16[8,3072]{1,0:T(8,128)(2,1)S(1)}, bf16[8,3072]{1,0:T(8,128)(2,1)S(1)}, u32[]{:S(2)}, u32[]{:S(2)}) collective-permute-start(bf16[8,3072]{1,0:T(8,128)(2,1)S(1)} %get-tuple-element.12), channel_id=1, source_target_pairs={{32,0},{64,32},{96,64},{33,1},{65,33},{97,65},{34,2},{66,34},{98,6... | collective-permute-start | bytes 147464 | tf_op jit(solution)/shard_map/ppermute | solution.py:10
  504.7 39.0 %slice-start.10 = ((s8[6291456]{0:T(1024)(128)(4,1)}), s8[4194304]{0:T(1024)(128)(4,1)S(1)}, s32[]{:S(2)}) async-start(s8[6291456]{0:T(1024)(128)(4,1)} %bitcast.258), calls=%async_computation.26 | async-start | bytes 8388608
  543.8 10.5 %copy-start.26 = (bf16[64,1024]{1,0:T(8,128)(2,1)S(1)}, bf16[64,1024]{1,0:T(8,128)(2,1)}, u32[]{:S(2)}) copy-start(bf16[64,1024]{1,0:T(8,128)(2,1)} %copy-done.25) | copy-start | bytes 393220
  546.6 224.0 %reduce-scatter.17.cloned.1.call-start = ((), (), s32[]{:S(2)}) async-start(), calls=%async_computation.12 | async-start | bytes 442368 | tf_op jit(solution)/shard_map/reduce_scatter | solution.py:72
  560.7 102.7 %slice-start.6 = ((s8[6291456]{0:T(1024)(128)(4,1)}), s8[2097152]{0:T(1024)(128)(4,1)S(1)}, s32[]{:S(2)}) async-start(s8[6291456]{0:T(1024)(128)(4,1)} %bitcast.254), calls=%async_computation.22 | async-start | bytes 4194304
  618.2 45.3 %copy-start.42 = (f32[64]{0:T(128)S(1)}, f32[64]{0:T(128)}, u32[]{:S(2)}) copy-start(f32[64]{0:T(128)} %get-tuple-element.4) | copy-start | bytes 772
  619.0 46.5 %slice-start.2 = ((s8[6291456]{0:T(1024)(128)(4,1)}), s8[4194304]{0:T(1024)(128)(4,1)S(1)}, s32[]{:S(2)}) async-start(s8[6291456]{0:T(1024)(128)(4,1)} %bitcast.250), calls=%async_computation.18 | async-start | bytes 8388608
  619.0 44.4 %slice-start.7 = ((s8[6291456]{0:T(1024)(128)(4,1)}), s8[4194304]{0:T(1024)(128)(4,1)S(1)}, s32[]{:S(2)}) async-start(s8[6291456]{0:T(1024)(128)(4,1)} %bitcast.254), calls=%async_computation.23 | async-start | bytes 8388608
  619.1 46.5 %slice-start.3 = ((s8[6291456]{0:T(1024)(128)(4,1)}), s8[2097152]{0:T(1024)(128)(4,1)S(1)}, s32[]{:S(2)}) async-start(s8[6291456]{0:T(1024)(128)(4,1)} %bitcast.250), calls=%async_computation.19 | async-start | bytes 4194304
  619.1 9.6 %collective-permute-start.4 = (bf16[8,3072]{1,0:T(8,128)(2,1)S(1)}, bf16[8,3072]{1,0:T(8,128)(2,1)S(1)}, u32[]{:S(2)}, u32[]{:S(2)}) collective-permute-start(bf16[8,3072]{1,0:T(8,128)(2,1)S(1)} %get-tuple-element.10), channel_id=1, source_target_pairs={{32,0},{64,32},{96,64},{33,1},{65,33},{97,65},{34,2},{66,34},{98,6... | collective-permute-start | bytes 147464 | tf_op jit(solution)/shard_map/ppermute | solution.py:10
  628.6 39.0 %slice-start.12 = ((s8[6291456]{0:T(1024)(128)(4,1)}), s8[4194304]{0:T(1024)(128)(4,1)S(1)}, s32[]{:S(2)}) async-start(s8[6291456]{0:T(1024)(128)(4,1)} %bitcast.260), calls=%async_computation.28 | async-start | bytes 8388608
  670.5 20.8 %copy-start.15 = (bf16[64,1024]{1,0:T(8,128)(2,1)S(1)}, bf16[64,1024]{1,0:T(8,128)(2,1)}, u32[]{:S(2)}) copy-start(bf16[64,1024]{1,0:T(8,128)(2,1)} %copy-done.14) | copy-start | bytes 393220
  670.5 136.9 %reduce-scatter.19.cloned.1.call-start = ((), (), s32[]{:S(2)}) async-start(), calls=%async_computation.13 | async-start | bytes 7864320 | tf_op jit(solution)/shard_map/reduce_scatter | solution.py:89
  690.8 183.3 %reduce-scatter.21.cloned.1.call-start = ((), (), s32[]{:S(2)}) async-start(), calls=%async_computation.14 | async-start | bytes 7864320 | tf_op jit(solution)/shard_map/reduce_scatter | solution.py:92
  714.3 17.0 %copy-start.7 = (bf16[64,3072]{1,0:T(8,128)(2,1)S(1)}, bf16[64,3072]{1,0:T(8,128)(2,1)}, u32[]{:S(2)}) copy-start(bf16[64,3072]{1,0:T(8,128)(2,1)} %copy-done.6) | copy-start | bytes 1179652
  714.3 17.0 %copy-start.41 = (f32[64]{0:T(128)S(1)}, f32[64]{0:T(128)}, u32[]{:S(2)}) copy-start(f32[64]{0:T(128)} %copy-done.40) | copy-start | bytes 772
  731.1 209.8 %reduce-scatter.23.cloned.1.call-start = ((), (), s32[]{:S(2)}) async-start(), calls=%async_computation.15 | async-start | bytes 7864320 | tf_op jit(solution)/shard_map/reduce_scatter | solution.py:96
  733.2 13.0 %copy-start.13 = (bf16[64,3072]{1,0:T(8,128)(2,1)S(1)}, bf16[64,3072]{1,0:T(8,128)(2,1)}, u32[]{:S(2)}) copy-start(bf16[64,3072]{1,0:T(8,128)(2,1)} %copy-done.12) | copy-start | bytes 1179652
  733.2 13.0 %copy-start.35 = (f32[64]{0:T(128)S(1)}, f32[64]{0:T(128)}, u32[]{:S(2)}) copy-start(f32[64]{0:T(128)} %get-tuple-element.8) | copy-start | bytes 772
  739.7 13.7 %copy-start.5 = (bf16[64,3072]{1,0:T(8,128)(2,1)S(1)}, bf16[64,3072]{1,0:T(8,128)(2,1)}, u32[]{:S(2)}) copy-start(bf16[64,3072]{1,0:T(8,128)(2,1)} %copy-done.4) | copy-start | bytes 1179652
  739.7 13.7 %copy-start.43 = (f32[64]{0:T(128)S(1)}, f32[64]{0:T(128)}, u32[]{:S(2)}) copy-start(f32[64]{0:T(128)} %get-tuple-element.4) | copy-start | bytes 772
  771.4 169.4 %copy-start.33 = (bf16[1,2,8,3072]{3,2,1,0:T(8,128)(2,1)}, bf16[1,2,8,3072]{3,2,1,0:T(8,128)(2,1)S(1)}, u32[]{:S(2)}) copy-start(bf16[1,2,8,3072]{3,2,1,0:T(8,128)(2,1)S(1)} %fusion.160) | copy-start | bytes 294916
  (23 other events, 104.9 us)
Sparse Core Ops, SparseCore 0:
  60.8 73.1 reduce-scatter.8
  188.9 70.2 reduce-scatter.10
  313.8 70.4 reduce-scatter.12
  546.7 71.4 reduce-scatter.14
  670.6 70.5 reduce-scatter.16
  744.0 63.2 reduce-scatter.18
  810.3 63.7 reduce-scatter.20
  877.1 63.7 reduce-scatter.22
where the time goes:
time: 957 us; the launch traced here: 948 us
  waiting for transfers between devices  374 us (39%)
  blocking collectives  355 us (37%)
  matrix products  186 us (19%)
  between operations  15.1 us (2%)
    reduce_scatter x5, waiting for transfers between devices, shards(): lax.psum_scatter((first_term + lax.dot_general(d_up, up_w, (((1,), (1,)),...  201 us
    all_gather x5, blocking collectives, shards(): lax.all_gather(lax.dynamic_index_in_dim(layer_in[0], pick, 0, keepdims=Fa...  180 us
    all_gather x5, blocking collectives, shards(): grad_all = lax.all_gather(grad_now, 'node', axis=0, tiled=True)  174 us
    reduce_scatter x1, waiting for transfers between devices, shards(): lax.psum_scatter(acc_down.astype(jnp.bfloat16), 'dp', scatter_dimension=1...  66.7 us
    reduce_scatter x1, waiting for transfers between devices, shards(): lax.psum_scatter(acc_up.astype(jnp.bfloat16), 'dp', scatter_dimension=0,...  66.7 us
    dot_general x5, matrix products, shards(): lax.dot_general(inputs_now, d_gate, (((0,), (0,)), ((), ())), preferred_e...  50.2 us
    dot_general x5, matrix products, shards(): lax.dot_general(inputs_now, d_up, (((0,), (0,)), ((), ())), preferred_ele...  39.7 us
    dot_general x5, matrix products, shards(): lax.dot_general(hidden, grad_all, (((0,), (0,)), ((), ())), preferred_ele...  39.2 us
  transfers between devices with their start and end apart: 13, of which 9 were waited for; matrix products, arithmetic and copies ran while one was open for 14% of the time, Pallas kernels for 0%

commit v1 on v0

v1 whole, which is shorter than its diff:
```python
import jax
import jax.numpy as jnp
from jax import lax
from jax.experimental import pallas as pl
from jax.experimental.pallas import tpu as pltpu
from jax.sharding import PartitionSpec as P

MESH = pl.DeviceIdType.MESH
F32 = jnp.float32
BF16 = jnp.bfloat16
SECTIONS = 4
DP = 4
NODES = 8
MICRO = 2
OWN = 8
ROWS = OWN * NODES
ALL = ROWS * DP
WIDTH = 3072
HID = 1024
CB = WIDTH // NODES
DB = WIDTH // DP
WD_SLOTS = 4
WG_SLOTS = 6
OFFSETS = ((1, 2), (1, 1), (1, 3), (0, 2), (1, 0), (0, 1), (0, 3))


def near(n, offset):
    high, x = lax.div(n, 4), lax.rem(n, 4)
    return lax.rem(high + offset[0], 2) * 4 + lax.rem(x + offset[1], 4)


def dot(a, b):
    return lax.dot_general(a, b, (((1,), (0,)), ((), ())), preferred_element_type=F32)


def remote(src, dst, send, recv, **device):
    return pltpu.make_async_remote_copy(
        src_ref=src,
        dst_ref=dst,
        send_sem=send,
        recv_sem=recv,
        device_id=device,
        device_id_type=MESH,
    )


def body(
    grad_out, layer_in, gate_pre, up_pre, ids, route, w_gate, w_up, w_down,
    grad_in, g_gate, g_up, g_down,
    wd_raw, wg_raw, wdt, wgut,
    ids_v, route_v, lin_v, coef_v,
    go, dyg, prt, snd, dgu,
    gates, ups, backs, dys, dys_send,
    lsc, lx, lg, lin_t, hid_t, dga, dua,
    acc_g, acc_u, acc_d, out_g, out_u, out_d,
    ret, gi, fp, fs, fr,
    s_small, s_wd, s_wg, s_out,
    ss_go, rs_go, ss_sc, rs_sc, ss_ga, rs_ga,
    ss_gate, rs_gate, ss_up, rs_up, ss_lx, rs_lx, ss_lg, rs_lg,
    ss_b, rs_b, ss_dy, rs_dy, ss_ret, rs_ret, ss_f, rs_f,
):
    s = lax.axis_index("section")
    r = lax.axis_index("dp")
    n = lax.axis_index("node")
    above = lax.rem(s + 1, SECTIONS)
    below = lax.rem(s + SECTIONS - 1, SECTIONS)
    own_rows = pl.ds(pl.multiple_of(r * ROWS, ROWS), ROWS)

    def peer(k):
        return lax.rem(r + k, DP)

    barrier = pltpu.get_barrier_semaphore()
    for offset in OFFSETS:
        pl.semaphore_signal(
            barrier, inc=1, device_id={"node": near(n, offset)}, device_id_type=MESH
        )
    for k in range(1, DP):
        pl.semaphore_signal(barrier, inc=1, device_id={"dp": peer(k)}, device_id_type=MESH)

    @pl.when(s < SECTIONS - 1)
    def _():
        for j in range(NODES):
            pl.semaphore_signal(
                barrier, inc=1, device_id={"section": above, "node": j}, device_id_type=MESH
            )

    @pl.when(s > 0)
    def _():
        for j in range(NODES):
            pl.semaphore_signal(
                barrier, inc=1, device_id={"section": below, "node": j}, device_id_type=MESH
            )

    def load_wd(j):
        return pltpu.make_async_copy(
            w_down.at[:, pl.ds(j * CB, CB)], wd_raw.at[j % WD_SLOTS], s_wd.at[j]
        )

    def load_wg(j):
        ref = w_gate if j < NODES else w_up
        return pltpu.make_async_copy(
            ref.at[pl.ds((j % NODES) * CB, CB), :], wg_raw.at[j % WG_SLOTS], s_wg.at[j]
        )

    for j in range(WD_SLOTS):
        load_wd(j).start()
    small = [
        pltpu.make_async_copy(ids, ids_v, s_small.at[0]),
        pltpu.make_async_copy(route, route_v, s_small.at[1]),
        pltpu.make_async_copy(layer_in, lin_v, s_small.at[2]),
        pltpu.make_async_copy(gate_pre, gates.at[:, own_rows, :], s_small.at[3]),
        pltpu.make_async_copy(up_pre, ups.at[:, own_rows, :], s_small.at[4]),
        pltpu.make_async_copy(grad_out, go.at[n], s_small.at[5]),
    ]
    for copy in small:
        copy.start()
    for j in range(WG_SLOTS):
        load_wg(j).start()

    neighbours = jnp.minimum(s, 1) + jnp.minimum(SECTIONS - 1 - s, 1)
    pl.semaphore_wait(barrier, NODES - 1 + DP - 1 + neighbours * NODES)

    def send_go(q):
        return remote(
            grad_out, go.at[n], ss_go.at[q], rs_go.at[n], node=near(n, OFFSETS[q])
        )

    def send_gate(k):
        return remote(
            gate_pre, gates.at[:, own_rows, :], ss_gate.at[k], rs_gate.at[r], dp=peer(k)
        )

    def send_up(k):
        return remote(
            up_pre, ups.at[:, own_rows, :], ss_up.at[k], rs_up.at[r], dp=peer(k)
        )

    def send_lx(k):
        return remote(
            lsc.at[peer(k)], lx.at[r], ss_lx.at[k], rs_lx.at[r], dp=peer(k)
        )

    def send_lg(q):
        return remote(lx, lg.at[n], ss_lg.at[q], rs_lg.at[n], node=near(n, OFFSETS[q]))

    @pl.when(s == SECTIONS - 1)
    def _():
        for q in range(NODES - 1):
            send_go(q).start()

    for copy in small:
        copy.wait()
    diagonal = lax.broadcasted_iota(jnp.int32, (ROWS, ROWS), 0) == lax.broadcasted_iota(
        jnp.int32, (ROWS, ROWS), 1
    )
    for m in range(MICRO):
        across = jnp.sum(
            jnp.where(ids_v[m] == 0, route_v[m], jnp.float32(0.0)), axis=0, keepdims=True
        )
        coef_v[m * ROWS : (m + 1) * ROWS, :] = jnp.sum(
            jnp.where(diagonal, across, jnp.float32(0.0)), axis=1, keepdims=True
        )

    def exchange():
        scale = jnp.concatenate(
            [
                coef_v[pl.ds(pl.multiple_of(m * ROWS + n * OWN, OWN), OWN), :]
                for m in range(MICRO)
            ],
            axis=0,
        )
        for j in range(DP):
            lsc[j] = (lin_v[:, j * DB : (j + 1) * DB].astype(F32) * scale).astype(BF16)
        lx[r] = lsc[r]
        for k in range(1, DP):
            send_lx(k).start()
        for k in range(1, DP):
            send_gate(k).start()
        for k in range(1, DP):
            send_up(k).start()

    def gather_inputs():
        for k in range(1, DP):
            remote(lsc.at[0], lx.at[peer(k)], ss_lx.at[k], rs_lx.at[peer(k)], dp=peer(k)).wait_recv()
        for q in range(NODES - 1):
            send_lg(q).start()
        lg[n] = lx[...]

    def prepare():
        for offset in OFFSETS:
            j = near(n, offset)
            remote(lx, lg.at[j], ss_lg.at[0], rs_lg.at[j], node=j).wait_recv()
        for m in range(MICRO):
            rows = jnp.concatenate(
                [
                    lg[i, k, :, :].astype(F32)[m * OWN : (m + 1) * OWN]
                    for k in range(DP)
                    for i in range(NODES)
                ],
                axis=0,
            )
            lin_t[m] = rows.astype(BF16).T
        for k in range(1, DP):
            j = peer(k)
            rows = pl.ds(pl.multiple_of(j * ROWS, ROWS), ROWS)
            remote(gate_pre, gates.at[:, rows, :], ss_gate.at[k], rs_gate.at[j], dp=j).wait_recv()
            remote(up_pre, ups.at[:, rows, :], ss_up.at[k], rs_up.at[j], dp=j).wait_recv()
        for m in range(MICRO):
            for c in range(2):
                rows = pl.ds(c * 128, 128)
                g = gates[m, rows, :].astype(F32)
                hidden = (g * jax.nn.sigmoid(g) * ups[m, rows, :].astype(F32)).astype(BF16)
                hid_t[m, :, c * 128 : (c + 1) * 128] = hidden.T

    @pl.when(s < 2)
    def _():
        exchange()

    for j in range(NODES):
        load_wd(j).wait()
        wdt[j] = wd_raw[j % WD_SLOTS].T
        if j + WD_SLOTS < NODES:
            load_wd(j + WD_SLOTS).start()
    for j in range(2 * NODES):
        load_wg(j).wait()
        half = (j // NODES) * HID
        wgut[j % NODES, half : half + HID, :] = wg_raw[j % WG_SLOTS].T
        if j + WG_SLOTS < 2 * NODES:
            load_wg(j + WG_SLOTS).start()

    @pl.when(s < 2)
    def _():
        gather_inputs()
        prepare()

    def send_ga(m, q):
        return remote(
            dyg.at[m, n], dyg.at[m, n], ss_ga.at[m, q], rs_ga.at[m, n], node=near(n, OFFSETS[q])
        )

    def recv_ga(m, j):
        return remote(dyg.at[m, j], dyg.at[m, j], ss_ga.at[m, 0], rs_ga.at[m, j], node=j)

    @pl.when(s == SECTIONS - 1)
    def _():
        for offset in OFFSETS:
            j = near(n, offset)
            remote(grad_out, go.at[j], ss_go.at[0], rs_go.at[j], node=j).wait_recv()
        for j in range(NODES):
            block = go[:, :, j * CB : (j + 1) * CB].astype(F32)
            for m in range(MICRO):
                dyg[m, j] = (
                    block[:, m * OWN : (m + 1) * OWN, :].reshape(ROWS, CB).astype(BF16)
                )

    @pl.when(s < SECTIONS - 1)
    def _():
        for m in range(MICRO):
            total = jnp.zeros((ROWS, CB), F32)
            for j in range(NODES):
                remote(
                    snd.at[m, j], prt.at[m, j], ss_sc.at[m, j], rs_sc.at[m, j],
                    section=above, node=j,
                ).wait_recv()
                total = total + prt[m, j].astype(F32)
            dyg[m, n] = total.astype(BF16)
            for q in range(NODES - 1):
                send_ga(m, q).start()

    def send_sc(m, j):
        return remote(
            snd.at[m, j], prt.at[m, n], ss_sc.at[m, j], rs_sc.at[m, n], section=below, node=j
        )

    def send_b(m, k):
        return remote(
            backs.at[m, own_rows, :], backs.at[m, own_rows, :],
            ss_b.at[m, k], rs_b.at[m, r], dp=peer(k),
        )

    def send_dy(m, k):
        return remote(
            dys_send.at[m, k - 1], dys.at[m, :, own_rows, :],
            ss_dy.at[m, k], rs_dy.at[m, r], dp=peer(k),
        )

    def send_f(m, q):
        return remote(
            fs.at[m, q], fr.at[m, n], ss_f.at[m, q], rs_f.at[m, n], node=near(n, OFFSETS[q])
        )

    for m in range(MICRO):
        back = dot(dyg[m, n], wdt[n])
        for offset in OFFSETS[::-1]:
            j = near(n, offset)

            @pl.when(s < SECTIONS - 1)
            def _(j=j):
                recv_ga(m, j).wait_recv()

            back = back + dot(dyg[m, j], wdt[j])
        backs[m, own_rows, :] = back.astype(BF16)
        for k in range(1, DP):
            send_b(m, k).start()
        back = back * coef_v[m * ROWS : (m + 1) * ROWS, :]
        gate = gates[m, own_rows, :].astype(F32)
        sigma = jax.nn.sigmoid(gate)
        dgu[m, :, :HID] = (
            back * ups[m, own_rows, :].astype(F32) * sigma * (1.0 + gate * (1.0 - sigma))
        ).astype(BF16)
        dgu[m, :, HID:] = (back * gate * sigma).astype(BF16)
        for offset in OFFSETS + ((0, 0),):
            j = near(n, offset)
            part = dot(dgu[m], wgut[j])
            if offset == (0, 0):
                part = part + dyg[m, j].astype(F32)

            @pl.when(s > 0)
            def _(j=j, part=part):
                snd[m, j] = part.astype(BF16)
                send_sc(m, j).start()

            @pl.when(s == 0)
            def _(j=j, part=part):
                fp[j] = part.reshape(NODES, OWN, CB)

        @pl.when(s == 0)
        def _():
            def folded(i):
                return [
                    jnp.concatenate([fp[c, i], fp[c + NODES // 2, i]], axis=0).astype(BF16)
                    for c in range(NODES // 2)
                ]

            for q in range(NODES - 1):
                for c, value in enumerate(folded(near(n, OFFSETS[q]))):
                    fs[m, q, :, c * CB : (c + 1) * CB] = value
                send_f(m, q).start()
            for c, value in enumerate(folded(n)):
                fr[m, n, :, c * CB : (c + 1) * CB] = value

        scale = coef_v[m * ROWS : (m + 1) * ROWS, :]
        for k in range(DP):
            for h in range(2):
                value = (dyg[m, 2 * peer(k) + h].astype(F32) * scale).astype(BF16)
                if k == 0:
                    dys[m, h, own_rows, :] = value
                else:
                    dys_send[m, k - 1, h] = value
        for k in range(1, DP):
            send_dy(m, k).start()

    def send_ret():
        return remote(ret, gi, ss_ret.at[0], rs_ret.at[0], section=above)

    @pl.when(s < SECTIONS - 1)
    def _():
        window = pl.ds(pl.multiple_of(lax.div(n, 2) * 16, 16), 16)
        odd = lax.rem(n, 2) == 1
        for j in range(NODES):
            picked = []
            for m in range(MICRO):
                value = dyg[m, j, window, :].astype(F32)
                picked.append(jnp.where(odd, value[OWN:], value[:OWN]))
            ret[:, j * CB : (j + 1) * CB] = jnp.concatenate(picked, axis=0).astype(BF16)
        send_ret().start()

    @pl.when(s >= 2)
    def _():
        exchange()
        gather_inputs()
        prepare()

    def out_copy(which, i):
        staged, array = ((out_g, g_gate), (out_u, g_up), (out_d, g_down))[which]
        rows = pl.ds(i * 256, 256)
        return pltpu.make_async_copy(staged.at[rows, :], array.at[rows, :], s_out.at[which, i])

    for m in range(MICRO):
        for k in range(1, DP):
            j = peer(k)
            rows = pl.ds(pl.multiple_of(j * ROWS, ROWS), ROWS)
            remote(
                dys_send.at[m, 0], dys.at[m, :, rows, :], ss_dy.at[m, k], rs_dy.at[m, j], dp=j
            ).wait_recv()
        for i in range(HID // 256):
            rows = slice(i * 256, (i + 1) * 256)
            for h in range(2):
                cols = slice(h * CB, (h + 1) * CB)
                value = dot(hid_t[m, rows, :], dys[m, h])
                if m == 0:
                    acc_d[rows, cols] = value
                else:
                    out_d[rows, cols] = (acc_d[rows, cols] + value).astype(BF16)
            if m == 1:
                out_copy(2, i).start()
        for k in range(1, DP):
            j = peer(k)
            rows = pl.ds(pl.multiple_of(j * ROWS, ROWS), ROWS)
            remote(
                backs.at[m, own_rows, :], backs.at[m, rows, :], ss_b.at[m, k], rs_b.at[m, j], dp=j
            ).wait_recv()
        for k in range(DP):
            rows = slice(k * ROWS, (k + 1) * ROWS)
            back = backs[m, rows, :].astype(F32)
            gate = gates[m, rows, :].astype(F32)
            sigma = jax.nn.sigmoid(gate)
            dga[rows, :] = (
                back * ups[m, rows, :].astype(F32) * sigma * (1.0 + gate * (1.0 - sigma))
            ).astype(BF16)
            dua[rows, :] = (back * gate * sigma).astype(BF16)
        for which, (d, acc, out) in enumerate(((dga, acc_g, out_g), (dua, acc_u, out_u))):
            for i in range(DB // 256):
                rows = slice(i * 256, (i + 1) * 256)
                value = dot(lin_t[m, rows, :], d[...])
                if m == 0:
                    acc[rows, :] = value
                else:
                    out[rows, :] = (acc[rows, :] + value).astype(BF16)
                    out_copy(which, i).start()

    @pl.when(s == 0)
    def _():
        totals = []
        for m in range(MICRO):
            for offset in OFFSETS:
                j = near(n, offset)
                remote(fs.at[m, 0], fr.at[m, j], ss_f.at[m, 0], rs_f.at[m, j], node=j).wait_recv()
            total = jnp.zeros((16, WIDTH // 2), F32)
            for j in range(NODES):
                total = total + fr[m, j].astype(F32)
            totals.append(total)
        for c in range(2):
            gi[:, c * (WIDTH // 2) : (c + 1) * (WIDTH // 2)] = jnp.concatenate(
                [total[c * OWN : (c + 1) * OWN] for total in totals], axis=0
            ).astype(BF16)

    @pl.when(s > 0)
    def _():
        remote(ret, gi, ss_ret.at[0], rs_ret.at[0], section=below).wait_recv()

    last = pltpu.make_async_copy(gi, grad_in, s_small.at[6])
    last.start()

    @pl.when(s == SECTIONS - 1)
    def _():
        for q in range(NODES - 1):
            send_go(q).wait_send()

    for k in range(1, DP):
        send_gate(k).wait_send()
        send_up(k).wait_send()
        send_lx(k).wait_send()
    for q in range(NODES - 1):
        send_lg(q).wait_send()
    for m in range(MICRO):
        for k in range(1, DP):
            send_b(m, k).wait_send()
            send_dy(m, k).wait_send()

    @pl.when(s < SECTIONS - 1)
    def _():
        for m in range(MICRO):
            for q in range(NODES - 1):
                send_ga(m, q).wait_send()
        send_ret().wait_send()

    @pl.when(s > 0)
    def _():
        for m in range(MICRO):
            for j in range(NODES):
                send_sc(m, j).wait_send()

    @pl.when(s == 0)
    def _():
        for m in range(MICRO):
            for q in range(NODES - 1):
                send_f(m, q).wait_send()

    for which, count in ((0, DB // 256), (1, DB // 256), (2, HID // 256)):
        for i in range(count):
            out_copy(which, i).wait()
    last.wait()


def shards(grad_out, layer_in, gate_pre, up_pre, expert_ids, route_weight, w_gate, w_up, w_down):
    both = MICRO * OWN
    dma = pltpu.SemaphoreType.DMA
    vmem = pltpu.VMEM
    scratch = [
        vmem((WD_SLOTS, HID, CB), BF16),
        vmem((WG_SLOTS, CB, HID), BF16),
        vmem((NODES, CB, HID), BF16),
        vmem((NODES, 2 * HID, CB), BF16),
        vmem((MICRO, 2, ROWS), jnp.int32),
        vmem((MICRO, 2, ROWS), F32),
        vmem((both, WIDTH), BF16),
        vmem((MICRO * ROWS, 1), F32),
        vmem((NODES, both, WIDTH), BF16),
        vmem((MICRO, NODES, ROWS, CB), BF16),
        vmem((MICRO, NODES, ROWS, CB), BF16),
        vmem((MICRO, NODES, ROWS, CB), BF16),
        vmem((MICRO, ROWS, 2 * HID), BF16),
        vmem((MICRO, ALL, HID), BF16),
        vmem((MICRO, ALL, HID), BF16),
        vmem((MICRO, ALL, HID), BF16),
        vmem((MICRO, 2, ALL, CB), BF16),
        vmem((MICRO, DP - 1, 2, ROWS, CB), BF16),
        vmem((DP, both, DB), BF16),
        vmem((DP, both, DB), BF16),
        vmem((NODES, DP, both, DB), BF16),
        vmem((MICRO, DB, ALL), BF16),
        vmem((MICRO, HID, ALL), BF16),
        vmem((ALL, HID), BF16),
        vmem((ALL, HID), BF16),
        vmem((DB, HID), F32),
        vmem((DB, HID), F32),
        vmem((HID, DB), F32),
        vmem((DB, HID), BF16),
        vmem((DB, HID), BF16),
        vmem((HID, DB), BF16),
        vmem((both, WIDTH), BF16),
        vmem((both, WIDTH), BF16),
        vmem((NODES, NODES, OWN, CB), F32),
        vmem((MICRO, NODES - 1, 16, WIDTH // 2), BF16),
        vmem((MICRO, NODES, 16, WIDTH // 2), BF16),
        dma((7,)),
        dma((NODES,)),
        dma((2 * NODES,)),
        dma((3, 4)),
        dma((NODES,)),
        dma((NODES,)),
        dma((MICRO, NODES)),
        dma((MICRO, NODES)),
        dma((MICRO, NODES)),
        dma((MICRO, NODES)),
        dma((DP,)),
        dma((DP,)),
        dma((DP,)),
        dma((DP,)),
        dma((DP,)),
        dma((DP,)),
        dma((NODES,)),
        dma((NODES,)),
        dma((MICRO, DP)),
        dma((MICRO, DP)),
        dma((MICRO, DP)),
        dma((MICRO, DP)),
        dma((1,)),
        dma((1,)),
        dma((MICRO, NODES)),
        dma((MICRO, NODES)),
    ]
    anywhere = pl.BlockSpec(memory_space=pl.ANY)
    grad_in, g_gate, g_up, g_down = pl.pallas_call(
        body,
        out_shape=(
            jax.ShapeDtypeStruct((both, WIDTH), BF16),
            jax.ShapeDtypeStruct((DB, HID), BF16),
            jax.ShapeDtypeStruct((DB, HID), BF16),
            jax.ShapeDtypeStruct((HID, DB), BF16),
        ),
        in_specs=[anywhere] * 9,
        out_specs=(anywhere,) * 4,
        scratch_shapes=scratch,
        compiler_params=pltpu.CompilerParams(
            collective_id=0, has_side_effects=True, vmem_limit_bytes=62 * 2**20
        ),
        cost_estimate=pl.CostEstimate(flops=5 * 10**9, bytes_accessed=24 * 10**6, transcendentals=10**6),
        name="relay",
    )(
        grad_out.reshape(both, WIDTH),
        layer_in.reshape(both, WIDTH),
        gate_pre[0],
        up_pre[0],
        expert_ids[0].transpose(0, 2, 1),
        route_weight[0].transpose(0, 2, 1),
        w_gate[0],
        w_up[0],
        w_down[0],
    )
    return grad_in.reshape(1, MICRO, OWN, WIDTH), g_gate[None], g_up[None], g_down[None]


def solution(mesh):
    return jax.shard_map(
        shards,
        mesh=mesh,
        in_specs=(
            P(None, ("dp", "node"), None),
            P("section", None, ("dp", "node"), None),
            P("section", None, "dp", "node"),
            P("section", None, "dp", "node"),
            P("section", None, "dp", None),
            P("section", None, "dp", None),
            P("section", None, "node"),
            P("section", None, "node"),
            P("section", "node", None),
        ),
        out_specs=(
            P("section", None, ("dp", "node"), None),
            P("section", "dp", "node"),
            P("section", "dp", "node"),
            P("section", "node", "dp"),
        ),
        check_vma=False,
    )
```

time: 957 us -> 92.7 us (0.10)
  waiting for transfers between devices: 374 us -> 0 us
  blocking collectives: 355 us -> 0 us
  matrix products: 186 us -> 0 us
  Pallas kernels: 0 us -> 84.4 us
  between operations: 15.1 us -> 0.65 us
    reduce_scatter x8 -> x0, waiting for transfers between devices: 371 us -> none  [the longest x5 201 us: shards(): lax.psum_scatter((first_term + lax.dot_general(d_up, up_w, (((1,), (1,)),...]
    all_gather x10 -> x0, blocking collectives: 355 us -> none  [the longest x5 180 us: shards(): lax.all_gather(lax.dynamic_index_in_dim(layer_in[0], pick, 0, keepdims=Fa...]
    dot_general x30 -> x0, matrix products: 186 us -> none  [the longest x5 50.2 us: shards(): lax.dot_general(inputs_now, d_gate, (((0,), (0,)), ((), ())), preferred_e...]
    pallas_call x0 -> x1, Pallas kernels: none -> 84.4 us  [shards(): pl.pallas_call(body, out_shape=(jax.ShapeDtypeStruct((both, WIDTH), BF16)...]
  transfers between devices with their start and end apart: 13 -> 0, of which waited for: 9 -> 0; matrix products, arithmetic and copies ran while one was open for 14% -> 0% of each run, Pallas kernels for 0% -> 0%
where the time goes in v1:
time: 92.7 us; the launch traced here: 92.5 us
  Pallas kernels  84.4 us (91%)
  local copies, waits for them, and re-layouts  7.45 us (8%)
    pallas_call x1, Pallas kernels, shards(): pl.pallas_call(body, out_shape=(jax.ShapeDtypeStruct((both, WIDTH), BF16)...  84.4 us
    unnamed x8, local copies, waits for them, and re-layouts  7.45 us

profile of v1, /device:TPU:0, one launch (start us, length us, event | category | flops | bytes accessed | tf_op | source)
XLA Modules:
  0.0 92.5 jit_solution(6729361078061091458)
XLA Ops:
  0.6 84.4 %relay.1 = (bf16[16,3072]{1,0:T(8,128)(2,1)}, bf16[768,1024]{1,0:T(8,128)(2,1)}, bf16[768,1024]{1,0:T(8,128)(2,1)}, bf16[1024,768]{1,0:T(8,128)(2,1)}) custom-call(bf16[16,3072]{1,0:T(8,128)(2,1)} %bitcast.25, bf16[16,3072]{1,0:T(8,128)(2,1)} %bitcast.26, bf16[2,64,1024]{2,1,0:T(8,128)(2,1)} %bitcast.23, bf16[2,64,1024]{2,1,0:T(8,128)(2,1)} %bitcast.24, ...), custom_call_target="tpu_custom_call" | custom-call | flops 5000000000 | bytes 24000000 | tf_op jit(solution)/shard_map/relay/pallas_call | solution.py:555
  85.0 1.5 %copy.17 = bf16[1,2,8,3072]{3,2,1,0:T(8,128)(2,1)} copy(bf16[1,2,8,3072]{3,2,1,0:T(8,128)(2,1)} %bitcast.27) | data formatting | bytes 196608
  86.6 0.0 copy-start.1
  86.6 2.8 %copy.18 = bf16[1,768,1024]{2,1,0:T(8,128)(2,1)} copy(bf16[1,768,1024]{2,1,0:T(8,128)(2,1)} %bitcast.22) | data formatting | bytes 3145728
  89.4 0.0 copy-done.1
  89.4 0.0 copy-start
  89.4 1.1 %copy.19 = bf16[1,768,1024]{2,1,0:T(8,128)(2,1)} copy(bf16[1,768,1024]{2,1,0:T(8,128)(2,1)S(1)} %bitcast.21) | data formatting | bytes 3145728
  90.5 0.8 copy-done
  91.3 1.1 %copy.20 = bf16[1,1024,768]{2,1,0:T(8,128)(2,1)} copy(bf16[1,1024,768]{2,1,0:T(8,128)(2,1)S(1)} %bitcast.20) | data formatting | bytes 3145728
Async XLA Ops:
  86.6 2.8 %copy-start.1 = (bf16[768,1024]{1,0:T(8,128)(2,1)S(1)}, bf16[768,1024]{1,0:T(8,128)(2,1)}, u32[]{:S(2)}) copy-start(bf16[768,1024]{1,0:T(8,128)(2,1)} %get-tuple-element.10) | copy-start | bytes 4718596
  89.4 2.0 %copy-start = (bf16[1024,768]{1,0:T(8,128)(2,1)S(1)}, bf16[1024,768]{1,0:T(8,128)(2,1)}, u32[]{:S(2)}) copy-start(bf16[1024,768]{1,0:T(8,128)(2,1)} %get-tuple-element.11) | copy-start | bytes 4718596

commit v2 on v1

--- a/solution.py
+++ b/solution.py
@@ -19,9 +19,8 @@
 HID = 1024
 CB = WIDTH // NODES
 DB = WIDTH // DP
-WD_SLOTS = 4
-WG_SLOTS = 6
-OFFSETS = ((1, 2), (1, 1), (1, 3), (0, 2), (1, 0), (0, 1), (0, 3))
+HALF = WIDTH // 2
+OFFSETS = ((1, 2), (1, 1), (1, 3), (1, 0), (0, 2), (0, 1), (0, 3))
 
 
 def near(n, offset):
@@ -46,13 +45,12 @@
 
 def body(
     grad_out, layer_in, gate_pre, up_pre, ids, route, w_gate, w_up, w_down,
-    grad_in, g_gate, g_up, g_down,
+    grad_in, lin_out, dg_out, du_out, gd_out,
     wd_raw, wg_raw, wdt, wgut,
-    ids_v, route_v, lin_v, coef_v,
+    ids_v, route_v, lin_v, coef_v, factors,
     go, dyg, prt, snd, dgu,
     gates, ups, backs, dys, dys_send,
-    lsc, lx, lg, lin_t, hid_t, dga, dua,
-    acc_g, acc_u, acc_d, out_g, out_u, out_d,
+    lsc, lx, lg, lin_t, hid_t, dga, dua, gd,
     ret, gi, fp, fs, fr,
     s_small, s_wd, s_wg, s_out,
     ss_go, rs_go, ss_sc, rs_sc, ss_ga, rs_ga,
@@ -91,19 +89,27 @@
                 barrier, inc=1, device_id={"section": below, "node": j}, device_id_type=MESH
             )
 
+    far = lax.rem(s + 2, SECTIONS)
+
+    @pl.when(lax.rem(s, 2) == 1)
+    def _():
+        for offset in OFFSETS:
+            pl.semaphore_signal(
+                barrier,
+                inc=1,
+                device_id={"section": far, "node": near(n, offset)},
+                device_id_type=MESH,
+            )
+
     def load_wd(j):
+        return pltpu.make_async_copy(w_down.at[:, pl.ds(j * CB, CB)], wd_raw.at[j], s_wd.at[j])
+
+    def load_wg(j):
+        ref = w_gate if j % 2 == 0 else w_up
         return pltpu.make_async_copy(
-            w_down.at[:, pl.ds(j * CB, CB)], wd_raw.at[j % WD_SLOTS], s_wd.at[j]
-        )
-
-    def load_wg(j):
-        ref = w_gate if j < NODES else w_up
-        return pltpu.make_async_copy(
-            ref.at[pl.ds((j % NODES) * CB, CB), :], wg_raw.at[j % WG_SLOTS], s_wg.at[j]
-        )
-
-    for j in range(WD_SLOTS):
-        load_wd(j).start()
+            ref.at[pl.ds((j // 2) * CB, CB), :], wg_raw.at[j], s_wg.at[j]
+        )
+
     small = [
         pltpu.make_async_copy(ids, ids_v, s_small.at[0]),
         pltpu.make_async_copy(route, route_v, s_small.at[1]),
@@ -114,15 +120,22 @@
     ]
     for copy in small:
         copy.start()
-    for j in range(WG_SLOTS):
+    for j in range(NODES):
+        load_wd(j).start()
+    for j in range(2 * NODES):
         load_wg(j).start()
 
     neighbours = jnp.minimum(s, 1) + jnp.minimum(SECTIONS - 1 - s, 1)
-    pl.semaphore_wait(barrier, NODES - 1 + DP - 1 + neighbours * NODES)
-
-    def send_go(q):
-        return remote(
-            grad_out, go.at[n], ss_go.at[q], rs_go.at[n], node=near(n, OFFSETS[q])
+    pl.semaphore_wait(
+        barrier,
+        NODES - 1 + DP - 1 + neighbours * NODES + lax.rem(s, 2) * (NODES - 1),
+    )
+
+    def send_go(q, half):
+        columns = pl.ds(half * HALF, HALF)
+        return remote(
+            grad_out.at[:, columns], go.at[n, :, columns], ss_go.at[q], rs_go.at[n, half],
+            section=SECTIONS - 1, node=near(n, OFFSETS[q]),
         )
 
     def send_gate(k):
@@ -146,7 +159,12 @@
     @pl.when(s == SECTIONS - 1)
     def _():
         for q in range(NODES - 1):
-            send_go(q).start()
+            send_go(q, 0).start()
+
+    @pl.when(s == 1)
+    def _():
+        for q in range(NODES - 1):
+            send_go(q, 1).start()
 
     for copy in small:
         copy.wait()
@@ -161,6 +179,14 @@
             jnp.where(diagonal, across, jnp.float32(0.0)), axis=1, keepdims=True
         )
 
+    for m in range(MICRO):
+        gate = gates[m, own_rows, :].astype(F32)
+        active = jax.nn.sigmoid(gate) * coef_v[m * ROWS : (m + 1) * ROWS, :]
+        factors[m, :, :HID] = (
+            ups[m, own_rows, :].astype(F32) * active * (1.0 + gate * (1.0 - jax.nn.sigmoid(gate)))
+        )
+        factors[m, :, HID:] = gate * active
+
     def exchange():
         scale = jnp.concatenate(
             [
@@ -185,6 +211,9 @@
         for q in range(NODES - 1):
             send_lg(q).start()
         lg[n] = lx[...]
+
+    def keep_lin():
+        return pltpu.make_async_copy(lin_t, lin_out, s_out.at[0])
 
     def prepare():
         for offset in OFFSETS:
@@ -199,7 +228,8 @@
                 ],
                 axis=0,
             )
-            lin_t[m] = rows.astype(BF16).T
+            lin_t[:, m * ALL : (m + 1) * ALL] = rows.astype(BF16).T
+        keep_lin().start()
         for k in range(1, DP):
             j = peer(k)
             rows = pl.ds(pl.multiple_of(j * ROWS, ROWS), ROWS)
@@ -210,7 +240,7 @@
                 rows = pl.ds(c * 128, 128)
                 g = gates[m, rows, :].astype(F32)
                 hidden = (g * jax.nn.sigmoid(g) * ups[m, rows, :].astype(F32)).astype(BF16)
-                hid_t[m, :, c * 128 : (c + 1) * 128] = hidden.T
+                hid_t[:, m * ALL + c * 128 : m * ALL + (c + 1) * 128] = hidden.T
 
     @pl.when(s < 2)
     def _():
@@ -218,15 +248,12 @@
 
     for j in range(NODES):
         load_wd(j).wait()
-        wdt[j] = wd_raw[j % WD_SLOTS].T
-        if j + WD_SLOTS < NODES:
-            load_wd(j + WD_SLOTS).start()
-    for j in range(2 * NODES):
-        load_wg(j).wait()
-        half = (j // NODES) * HID
-        wgut[j % NODES, half : half + HID, :] = wg_raw[j % WG_SLOTS].T
-        if j + WG_SLOTS < 2 * NODES:
-            load_wg(j + WG_SLOTS).start()
+        wdt[j] = wd_raw[j].T
+    for j in range(NODES):
+        load_wg(2 * j).wait()
+        load_wg(2 * j + 1).wait()
+        wgut[j, :HID, :] = wg_raw[2 * j].T
+        wgut[j, HID:, :] = wg_raw[2 * j + 1].T
 
     @pl.when(s < 2)
     def _():
@@ -241,27 +268,44 @@
     def recv_ga(m, j):
         return remote(dyg.at[m, j], dyg.at[m, j], ss_ga.at[m, 0], rs_ga.at[m, j], node=j)
 
+    def finish_back(m, back):
+        backs[m, own_rows, :] = back.astype(BF16)
+        dgu[m, :, :HID] = (back * factors[m, :, :HID]).astype(BF16)
+        dgu[m, :, HID:] = (back * factors[m, :, HID:]).astype(BF16)
+
+    def unpack(m, columns):
+        block = go[:, :, columns].astype(F32)
+        return block[:, m * OWN : (m + 1) * OWN, :].reshape(ROWS, CB).astype(BF16)
+
     @pl.when(s == SECTIONS - 1)
     def _():
-        for offset in OFFSETS:
-            j = near(n, offset)
-            remote(grad_out, go.at[j], ss_go.at[0], rs_go.at[j], node=j).wait_recv()
+        for half in range(2):
+            columns = pl.ds(half * HALF, HALF)
+            for offset in OFFSETS:
+                j = near(n, offset)
+                remote(
+                    grad_out.at[:, columns], go.at[j, :, columns], ss_go.at[0], rs_go.at[j, half],
+                    section=SECTIONS - 1, node=j,
+                ).wait_recv()
+        back = jnp.zeros((MICRO * ROWS, HID), F32)
         for j in range(NODES):
-            block = go[:, :, j * CB : (j + 1) * CB].astype(F32)
-            for m in range(MICRO):
-                dyg[m, j] = (
-                    block[:, m * OWN : (m + 1) * OWN, :].reshape(ROWS, CB).astype(BF16)
-                )
+            block = go[:, :, j * CB : (j + 1) * CB].reshape(MICRO * ROWS, CB)
+            back = back + dot(block, wdt[j])
+        back = back.reshape(NODES, MICRO * OWN, HID)
+        for m in range(MICRO):
+            finish_back(m, back[:, m * OWN : (m + 1) * OWN, :].reshape(ROWS, HID))
+            dyg[m, n] = unpack(m, pl.ds(pl.multiple_of(n * CB, CB), CB))
 
     @pl.when(s < SECTIONS - 1)
     def _():
         for m in range(MICRO):
-            total = jnp.zeros((ROWS, CB), F32)
             for j in range(NODES):
                 remote(
                     snd.at[m, j], prt.at[m, j], ss_sc.at[m, j], rs_sc.at[m, j],
                     section=above, node=j,
                 ).wait_recv()
+            total = prt[m, 0].astype(F32)
+            for j in range(1, NODES):
                 total = total + prt[m, j].astype(F32)
             dyg[m, n] = total.astype(BF16)
             for q in range(NODES - 1):
@@ -284,61 +328,28 @@
             ss_dy.at[m, k], rs_dy.at[m, r], dp=peer(k),
         )
 
-    def send_f(m, q):
-        return remote(
-            fs.at[m, q], fr.at[m, n], ss_f.at[m, q], rs_f.at[m, n], node=near(n, OFFSETS[q])
-        )
-
-    for m in range(MICRO):
-        back = dot(dyg[m, n], wdt[n])
-        for offset in OFFSETS[::-1]:
-            j = near(n, offset)
-
-            @pl.when(s < SECTIONS - 1)
-            def _(j=j):
-                recv_ga(m, j).wait_recv()
-
-            back = back + dot(dyg[m, j], wdt[j])
-        backs[m, own_rows, :] = back.astype(BF16)
-        for k in range(1, DP):
-            send_b(m, k).start()
-        back = back * coef_v[m * ROWS : (m + 1) * ROWS, :]
-        gate = gates[m, own_rows, :].astype(F32)
-        sigma = jax.nn.sigmoid(gate)
-        dgu[m, :, :HID] = (
-            back * ups[m, own_rows, :].astype(F32) * sigma * (1.0 + gate * (1.0 - sigma))
-        ).astype(BF16)
-        dgu[m, :, HID:] = (back * gate * sigma).astype(BF16)
-        for offset in OFFSETS + ((0, 0),):
-            j = near(n, offset)
-            part = dot(dgu[m], wgut[j])
-            if offset == (0, 0):
-                part = part + dyg[m, j].astype(F32)
-
-            @pl.when(s > 0)
-            def _(j=j, part=part):
-                snd[m, j] = part.astype(BF16)
-                send_sc(m, j).start()
-
-            @pl.when(s == 0)
-            def _(j=j, part=part):
-                fp[j] = part.reshape(NODES, OWN, CB)
-
-        @pl.when(s == 0)
-        def _():
-            def folded(i):
-                return [
-                    jnp.concatenate([fp[c, i], fp[c + NODES // 2, i]], axis=0).astype(BF16)
-                    for c in range(NODES // 2)
-                ]
-
-            for q in range(NODES - 1):
-                for c, value in enumerate(folded(near(n, OFFSETS[q]))):
-                    fs[m, q, :, c * CB : (c + 1) * CB] = value
-                send_f(m, q).start()
-            for c, value in enumerate(folded(n)):
-                fr[m, n, :, c * CB : (c + 1) * CB] = value
-
+    def send_f(m, q, step):
+        half = (1 - lax.div(n, 4)) if step == 0 else lax.div(n, 4)
+        return remote(
+            fs.at[m, q, step], fr.at[m, n, half], ss_f.at[m, q, step], rs_f.at[m, n, half],
+            node=near(n, OFFSETS[q]),
+        )
+
+    def send_tokens(m, step):
+        half = (1 - lax.div(n, 4)) if step == 0 else lax.div(n, 4)
+
+        def put(place, i):
+            for c in range(2):
+                place[:, c * CB : (c + 1) * CB] = jnp.concatenate(
+                    [fp[half * 4 + c, i], fp[half * 4 + 2 + c, i]], axis=0
+                ).astype(BF16)
+
+        for q in range(NODES - 1):
+            put(fs.at[m, q, step], near(n, OFFSETS[q]))
+            send_f(m, q, step).start()
+        put(fr.at[m, n, half], n)
+
+    def exchange_dy(m):
         scale = coef_v[m * ROWS : (m + 1) * ROWS, :]
         for k in range(DP):
             for h in range(2):
@@ -349,6 +360,61 @@
                     dys_send[m, k - 1, h] = value
         for k in range(1, DP):
             send_dy(m, k).start()
+
+    arrivals = (((0, 1), (0, 3)), ((0, 2), (1, 0)), ((1, 1), (1, 3), (1, 2)))
+    order = OFFSETS + ((0, 0),)
+    for m in range(MICRO):
+
+        @pl.when(s < SECTIONS - 1)
+        def _():
+            back = dot(dyg[m, n], wdt[n])
+            for group in arrivals:
+                for offset in group:
+                    recv_ga(m, near(n, offset)).wait_recv()
+                for offset in group:
+                    j = near(n, offset)
+                    back = back + dot(dyg[m, j], wdt[j])
+            finish_back(m, back)
+
+        @pl.when(s == 0)
+        def _():
+            for k in range(1, DP):
+                send_b(m, k).start()
+            exchange_dy(m)
+
+        for g in range(NODES // 2):
+            for offset in order[2 * g : 2 * g + 2]:
+                j = near(n, offset)
+                part = dot(dgu[m], wgut[j])
+                if offset == (0, 0):
+                    part = part + dyg[m, n].astype(F32)
+                snd[m, j] = part.astype(BF16)
+                fp[j] = part.reshape(NODES, OWN, CB)
+
+            @pl.when(s > 0)
+            def _():
+                for offset in order[2 * g : 2 * g + 2]:
+                    send_sc(m, near(n, offset)).start()
+
+            if g % 2 == 1:
+
+                @pl.when(s == 0)
+                def _():
+                    send_tokens(m, g // 2)
+
+    @pl.when(s == SECTIONS - 1)
+    def _():
+        for m in range(MICRO):
+            for j in range(NODES):
+                dyg[m, j] = unpack(m, slice(j * CB, (j + 1) * CB))
+
+    @pl.when(s > 0)
+    def _():
+        for m in range(MICRO):
+            for k in range(1, DP):
+                send_b(m, k).start()
+        for m in range(MICRO):
+            exchange_dy(m)
 
     def send_ret():
         return remote(ret, gi, ss_ret.at[0], rs_ret.at[0], section=above)
@@ -371,29 +437,15 @@
         gather_inputs()
         prepare()
 
-    def out_copy(which, i):
-        staged, array = ((out_g, g_gate), (out_u, g_up), (out_d, g_down))[which]
+    def keep_d(which, m):
+        staged, array = ((dga, dg_out), (dua, du_out))[which]
+        return pltpu.make_async_copy(staged.at[m], array.at[m], s_out.at[1 + 2 * which + m])
+
+    def keep_down(i):
         rows = pl.ds(i * 256, 256)
-        return pltpu.make_async_copy(staged.at[rows, :], array.at[rows, :], s_out.at[which, i])
-
-    for m in range(MICRO):
-        for k in range(1, DP):
-            j = peer(k)
-            rows = pl.ds(pl.multiple_of(j * ROWS, ROWS), ROWS)
-            remote(
-                dys_send.at[m, 0], dys.at[m, :, rows, :], ss_dy.at[m, k], rs_dy.at[m, j], dp=j
-            ).wait_recv()
-        for i in range(HID // 256):
-            rows = slice(i * 256, (i + 1) * 256)
-            for h in range(2):
-                cols = slice(h * CB, (h + 1) * CB)
-                value = dot(hid_t[m, rows, :], dys[m, h])
-                if m == 0:
-                    acc_d[rows, cols] = value
-                else:
-                    out_d[rows, cols] = (acc_d[rows, cols] + value).astype(BF16)
-            if m == 1:
-                out_copy(2, i).start()
+        return pltpu.make_async_copy(gd.at[rows, :], gd_out.at[rows, :], s_out.at[5 + i])
+
+    def spread(m):
         for k in range(1, DP):
             j = peer(k)
             rows = pl.ds(pl.multiple_of(j * ROWS, ROWS), ROWS)
@@ -405,35 +457,51 @@
             back = backs[m, rows, :].astype(F32)
             gate = gates[m, rows, :].astype(F32)
             sigma = jax.nn.sigmoid(gate)
-            dga[rows, :] = (
+            dga[m, rows, :] = (
                 back * ups[m, rows, :].astype(F32) * sigma * (1.0 + gate * (1.0 - sigma))
             ).astype(BF16)
-            dua[rows, :] = (back * gate * sigma).astype(BF16)
-        for which, (d, acc, out) in enumerate(((dga, acc_g, out_g), (dua, acc_u, out_u))):
-            for i in range(DB // 256):
-                rows = slice(i * 256, (i + 1) * 256)
-                value = dot(lin_t[m, rows, :], d[...])
-                if m == 0:
-                    acc[rows, :] = value
-                else:
-                    out[rows, :] = (acc[rows, :] + value).astype(BF16)
-                    out_copy(which, i).start()
+            dua[m, rows, :] = (back * gate * sigma).astype(BF16)
+        keep_d(0, m).start()
+        keep_d(1, m).start()
+
+    spread(0)
+    for m in range(MICRO):
+        for k in range(1, DP):
+            j = peer(k)
+            rows = pl.ds(pl.multiple_of(j * ROWS, ROWS), ROWS)
+            remote(
+                dys_send.at[m, 0], dys.at[m, :, rows, :], ss_dy.at[m, k], rs_dy.at[m, j], dp=j
+            ).wait_recv()
+    for i in range(HID // 256):
+        rows = slice(i * 256, (i + 1) * 256)
+        for h in range(2):
+            value = dot(hid_t[rows, :ALL], dys[0, h]) + dot(hid_t[rows, ALL:], dys[1, h])
+            gd[rows, h * CB : (h + 1) * CB] = value.astype(BF16)
+        keep_down(i).start()
+    spread(1)
 
     @pl.when(s == 0)
     def _():
-        totals = []
         for m in range(MICRO):
             for offset in OFFSETS:
                 j = near(n, offset)
-                remote(fs.at[m, 0], fr.at[m, j], ss_f.at[m, 0], rs_f.at[m, j], node=j).wait_recv()
-            total = jnp.zeros((16, WIDTH // 2), F32)
-            for j in range(NODES):
-                total = total + fr[m, j].astype(F32)
-            totals.append(total)
-        for c in range(2):
-            gi[:, c * (WIDTH // 2) : (c + 1) * (WIDTH // 2)] = jnp.concatenate(
-                [total[c * OWN : (c + 1) * OWN] for total in totals], axis=0
-            ).astype(BF16)
+                for half in range(2):
+                    remote(
+                        fs.at[m, 0, half], fr.at[m, j, half], ss_f.at[m, 0, half],
+                        rs_f.at[m, j, half], node=j,
+                    ).wait_recv()
+        for half in range(2):
+            totals = []
+            for m in range(MICRO):
+                total = fr[m, 0, half].astype(F32)
+                for j in range(1, NODES):
+                    total = total + fr[m, j, half].astype(F32)
+                totals.append(total)
+            for c in range(2):
+                start = half * HALF + c * 2 * CB
+                gi[:, start : start + 2 * CB] = jnp.concatenate(
+                    [total[c * OWN : (c + 1) * OWN] for total in totals], axis=0
+                ).astype(BF16)
 
     @pl.when(s > 0)
     def _():
@@ -445,7 +513,12 @@
     @pl.when(s == SECTIONS - 1)
     def _():
         for q in range(NODES - 1):
-            send_go(q).wait_send()
+            send_go(q, 0).wait_send()
+
+    @pl.when(s == 1)
+    def _():
+        for q in range(NODES - 1):
+            send_go(q, 1).wait_send()
 
     for k in range(1, DP):
         send_gate(k).wait_send()
@@ -475,12 +548,55 @@
     def _():
         for m in range(MICRO):
             for q in range(NODES - 1):
-                send_f(m, q).wait_send()
-
-    for which, count in ((0, DB // 256), (1, DB // 256), (2, HID // 256)):
-        for i in range(count):
-            out_copy(which, i).wait()
+                for step in range(2):
+                    send_f(m, q, step).wait_send()
+
+    keep_lin().wait()
+    for m in range(MICRO):
+        keep_d(0, m).wait()
+        keep_d(1, m).wait()
+    for i in range(HID // 256):
+        keep_down(i).wait()
     last.wait()
+
+
+def finish(
+    grad_in, lin, dg, du, down,
+    o_in, o_gate, o_up, o_down,
+    in_v, lin_v, dg_v, du_v, down_v, gate_v, up_v, sems,
+):
+    loads = [
+        pltpu.make_async_copy(lin, lin_v, sems.at[0]),
+        pltpu.make_async_copy(dg, dg_v, sems.at[1]),
+        pltpu.make_async_copy(du, du_v, sems.at[2]),
+        pltpu.make_async_copy(down, down_v, sems.at[3]),
+        pltpu.make_async_copy(grad_in, in_v, sems.at[4]),
+    ]
+    for copy in loads:
+        copy.start()
+    stores = []
+    loads[0].wait()
+    for which, (d, staged, out) in enumerate(((dg_v, gate_v, o_gate), (du_v, up_v, o_up))):
+        loads[1 + which].wait()
+        for i in range(DB // 256):
+            rows = pl.ds(i * 256, 256)
+            value = dot(lin_v[rows, :ALL], d[0]) + dot(lin_v[rows, ALL:], d[1])
+            staged[rows, :] = value.astype(BF16)
+            stores.append(
+                pltpu.make_async_copy(
+                    staged.at[rows, :], out.at[rows, :], sems.at[7 + 3 * which + i]
+                )
+            )
+            stores[-1].start()
+        if which == 0:
+            loads[3].wait()
+            loads[4].wait()
+            stores.append(pltpu.make_async_copy(down_v, o_down, sems.at[5]))
+            stores.append(pltpu.make_async_copy(in_v, o_in, sems.at[6]))
+            stores[-2].start()
+            stores[-1].start()
+    for copy in stores:
+        copy.wait()
 
 
 def shards(grad_out, layer_in, gate_pre, up_pre, expert_ids, route_weight, w_gate, w_up, w_down):
@@ -488,14 +604,15 @@
     dma = pltpu.SemaphoreType.DMA
     vmem = pltpu.VMEM
     scratch = [
-        vmem((WD_SLOTS, HID, CB), BF16),
-        vmem((WG_SLOTS, CB, HID), BF16),
+        vmem((NODES, HID, CB), BF16),
+        vmem((2 * NODES, CB, HID), BF16),
         vmem((NODES, CB, HID), BF16),
         vmem((NODES, 2 * HID, CB), BF16),
         vmem((MICRO, 2, ROWS), jnp.int32),
         vmem((MICRO, 2, ROWS), F32),
         vmem((both, WIDTH), BF16),
         vmem((MICRO * ROWS, 1), F32),
+        vmem((MICRO, ROWS, 2 * HID), F32),
         vmem((NODES, both, WIDTH), BF16),
         vmem((MICRO, NODES, ROWS, CB), BF16),
         vmem((MICRO, NODES, ROWS, CB), BF16),
@@ -509,27 +626,22 @@
         vmem((DP, both, DB), BF16),
         vmem((DP, both, DB), BF16),
         vmem((NODES, DP, both, DB), BF16),
-        vmem((MICRO, DB, ALL), BF16),
-        vmem((MICRO, HID, ALL), BF16),
-        vmem((ALL, HID), BF16),
-        vmem((ALL, HID), BF16),
-        vmem((DB, HID), F32),
-        vmem((DB, HID), F32),
-        vmem((HID, DB), F32),
-        vmem((DB, HID), BF16),
-        vmem((DB, HID), BF16),
+        vmem((DB, MICRO * ALL), BF16),
+        vmem((HID, MICRO * ALL), BF16),
+        vmem((MICRO, ALL, HID), BF16),
+        vmem((MICRO, ALL, HID), BF16),
         vmem((HID, DB), BF16),
         vmem((both, WIDTH), BF16),
         vmem((both, WIDTH), BF16),
         vmem((NODES, NODES, OWN, CB), F32),
-        vmem((MICRO, NODES - 1, 16, WIDTH // 2), BF16),
-        vmem((MICRO, NODES, 16, WIDTH // 2), BF16),
+        vmem((MICRO, NODES - 1, 2, 16, 2 * CB), BF16),
+        vmem((MICRO, NODES, 2, 16, 2 * CB), BF16),
         dma((7,)),
         dma((NODES,)),
         dma((2 * NODES,)),
-        dma((3, 4)),
+        dma((9,)),
         dma((NODES,)),
-        dma((NODES,)),
+        dma((NODES, 2)),
         dma((MICRO, NODES)),
         dma((MICRO, NODES)),
         dma((MICRO, NODES)),
@@ -548,20 +660,21 @@
         dma((MICRO, DP)),
         dma((1,)),
         dma((1,)),
-        dma((MICRO, NODES)),
-        dma((MICRO, NODES)),
+        dma((MICRO, NODES, 2)),
+        dma((MICRO, NODES, 2)),
     ]
     anywhere = pl.BlockSpec(memory_space=pl.ANY)
-    grad_in, g_gate, g_up, g_down = pl.pallas_call(
+    left = pl.pallas_call(
         body,
         out_shape=(
             jax.ShapeDtypeStruct((both, WIDTH), BF16),
-            jax.ShapeDtypeStruct((DB, HID), BF16),
-            jax.ShapeDtypeStruct((DB, HID), BF16),
+            jax.ShapeDtypeStruct((DB, MICRO * ALL), BF16),
+            jax.ShapeDtypeStruct((MICRO, ALL, HID), BF16),
+            jax.ShapeDtypeStruct((MICRO, ALL, HID), BF16),
             jax.ShapeDtypeStruct((HID, DB), BF16),
         ),
         in_specs=[anywhere] * 9,
-        out_specs=(anywhere,) * 4,
+        out_specs=(anywhere,) * 5,
         scratch_shapes=scratch,
         compiler_params=pltpu.CompilerParams(
             collective_id=0, has_side_effects=True, vmem_limit_bytes=62 * 2**20
@@ -579,6 +692,30 @@
         w_up[0],
         w_down[0],
     )
+    grad_in, g_gate, g_up, g_down = pl.pallas_call(
+        finish,
+        out_shape=(
+            jax.ShapeDtypeStruct((both, WIDTH), BF16),
+            jax.ShapeDtypeStruct((DB, HID), BF16),
+            jax.ShapeDtypeStruct((DB, HID), BF16),
+            jax.ShapeDtypeStruct((HID, DB), BF16),
+        ),
+        in_specs=[anywhere] * 5,
+        out_specs=(anywhere,) * 4,
+        scratch_shapes=[
+            vmem((both, WIDTH), BF16),
+            vmem((DB, MICRO * ALL), BF16),
+            vmem((MICRO, ALL, HID), BF16),
+            vmem((MICRO, ALL, HID), BF16),
+            vmem((HID, DB), BF16),
+            vmem((DB, HID), BF16),
+            vmem((DB, HID), BF16),
+            dma((13,)),
+        ],
+        compiler_params=pltpu.CompilerParams(vmem_limit_bytes=62 * 2**20),
+        cost_estimate=pl.CostEstimate(flops=16 * 10**8, bytes_accessed=10**7, transcendentals=0),
+        name="finish",
+    )(*left)
     return grad_in.reshape(1, MICRO, OWN, WIDTH), g_gate[None], g_up[None], g_down[None]
 
 

time: 92.7 us -> 86.8 us (0.936)
  local copies, waits for them, and re-layouts: 7.45 us -> 0 us
  Pallas kernels: 84.4 us -> 85.9 us
    unnamed x8 -> x0, local copies, waits for them, and re-layouts: 7.45 us -> none
    pallas_call x0 -> x1, Pallas kernels: none -> 4.43 us  [shards(): pl.pallas_call(finish, out_shape=(jax.ShapeDtypeStruct((both, WIDTH), BF1...]
    pallas_call x1, Pallas kernels: 84.4 us -> 81.5 us  [shards(): pl.pallas_call(body, out_shape=(jax.ShapeDtypeStruct((both, WIDTH), BF16)...]
where the time goes in v2:
time: 86.8 us; the launch traced here: 86.7 us
  Pallas kernels  85.9 us (99%)
    pallas_call x1, Pallas kernels, shards(): pl.pallas_call(body, out_shape=(jax.ShapeDtypeStruct((both, WIDTH), BF16)...  81.5 us
    pallas_call x1, Pallas kernels, shards(): pl.pallas_call(finish, out_shape=(jax.ShapeDtypeStruct((both, WIDTH), BF1...  4.43 us

profile of v2, /device:TPU:0, one launch (start us, length us, event | category | flops | bytes accessed | tf_op | source)
XLA Modules:
  0.0 86.7 jit_solution(17887222947316924836)
XLA Ops:
  0.6 81.5 %relay.1 = (bf16[16,3072]{1,0:T(8,128)(2,1)}, bf16[768,512]{1,0:T(8,128)(2,1)}, bf16[2,256,1024]{2,1,0:T(8,128)(2,1)}, bf16[2,256,1024]{2,1,0:T(8,128)(2,1)}, bf16[1024,768]{1,0:T(8,128)(2,1)}) custom-call(bf16[16,3072]{1,0:T(8,128)(2,1)} %bitcast.22, bf16[16,3072]{1,0:T(8,128)(2,1)} %bitcast.23, bf16[2,64,1024]{2,1,0:T(8,128)(2,1)} %bitcast.20, ...), custom_call_target="tpu_custom_call" | custom-call | flops 5000000000 | bytes 24000000 | tf_op jit(solution)/shard_map/relay/pallas_call | solution.py:667
  82.1 4.4 %finish.1 = (bf16[16,3072]{1,0:T(8,128)(2,1)}, bf16[768,1024]{1,0:T(8,128)(2,1)}, bf16[768,1024]{1,0:T(8,128)(2,1)}, bf16[1024,768]{1,0:T(8,128)(2,1)}) custom-call(bf16[16,3072]{1,0:T(8,128)(2,1)} %get-tuple-element.13.grad_in, bf16[768,512]{1,0:T(8,128)(2,1)} %get-tuple-element.14.lin, bf16[2,256,1024]{2,1,0:T(8,128)(2,1)} %get-tuple-element.15.dg, ...), custom_call_target="tpu_custom_call" | custom-call | flops 1600000000 | bytes 10000000 | tf_op jit(solution)/shard_map/finish/pallas_call | solution.py:695

commit v3 on v2

--- a/solution.py
+++ b/solution.py
@@ -20,6 +20,8 @@
 CB = WIDTH // NODES
 DB = WIDTH // DP
 HALF = WIDTH // 2
+WINDOW = 10
+PIECES = 3 * NODES
 OFFSETS = ((1, 2), (1, 1), (1, 3), (1, 0), (0, 2), (0, 1), (0, 3))
 
 
@@ -49,23 +51,60 @@
     wd_raw, wg_raw, wdt, wgut,
     ids_v, route_v, lin_v, coef_v, factors,
     go, dyg, prt, snd, dgu,
-    gates, ups, backs, dys, dys_send,
+    gates, ups, backs, dys, crow,
     lsc, lx, lg, lin_t, hid_t, dga, dua, gd,
     ret, gi, fp, fs, fr,
     s_small, s_wd, s_wg, s_out,
     ss_go, rs_go, ss_sc, rs_sc, ss_ga, rs_ga,
     ss_gate, rs_gate, ss_up, rs_up, ss_lx, rs_lx, ss_lg, rs_lg,
-    ss_b, rs_b, ss_dy, rs_dy, ss_ret, rs_ret, ss_f, rs_f,
+    ss_cr, rs_cr, ss_b, rs_b, ss_dy, rs_dy, ss_ret, rs_ret, ss_f, rs_f,
 ):
     s = lax.axis_index("section")
     r = lax.axis_index("dp")
     n = lax.axis_index("node")
     above = lax.rem(s + 1, SECTIONS)
     below = lax.rem(s + SECTIONS - 1, SECTIONS)
-    own_rows = pl.ds(pl.multiple_of(r * ROWS, ROWS), ROWS)
 
     def peer(k):
         return lax.rem(r + k, DP)
+
+    def load(i):
+        if i < NODES:
+            return pltpu.make_async_copy(
+                w_down.at[pl.ds(i * (HID // NODES), HID // NODES), :], wd_raw.at[i], s_wd.at[i]
+            )
+        j = i - NODES
+        ref = w_gate if j % 2 == 0 else w_up
+        return pltpu.make_async_copy(
+            ref.at[pl.ds((j // 2) * CB, CB), :], wg_raw.at[j], s_wg.at[j]
+        )
+
+    def turn(i):
+        load(i).wait()
+        if i + WINDOW < PIECES:
+            load(i + WINDOW).start()
+        if i < NODES:
+            rows = slice(i * (HID // NODES), (i + 1) * (HID // NODES))
+            for j in range(NODES):
+                wdt[j, :, rows] = wd_raw[i, :, j * CB : (j + 1) * CB].T
+        else:
+            j = i - NODES
+            start = (j % 2) * HID
+            wgut[j // 2, start : start + HID, :] = wg_raw[j].T
+
+    small = [
+        pltpu.make_async_copy(ids, ids_v, s_small.at[0]),
+        pltpu.make_async_copy(route, route_v, s_small.at[1]),
+        pltpu.make_async_copy(layer_in, lin_v, s_small.at[2]),
+        pltpu.make_async_copy(gate_pre, gates.at[r], s_small.at[3]),
+        pltpu.make_async_copy(up_pre, ups.at[r], s_small.at[4]),
+        pltpu.make_async_copy(grad_out.at[:, :HALF], go.at[n, 0], s_small.at[5]),
+        pltpu.make_async_copy(grad_out.at[:, HALF:], go.at[n, 1], s_small.at[6]),
+    ]
+    for copy in small:
+        copy.start()
+    for i in range(WINDOW):
+        load(i).start()
 
     barrier = pltpu.get_barrier_semaphore()
     for offset in OFFSETS:
@@ -100,71 +139,6 @@
                 device_id={"section": far, "node": near(n, offset)},
                 device_id_type=MESH,
             )
-
-    def load_wd(j):
-        return pltpu.make_async_copy(w_down.at[:, pl.ds(j * CB, CB)], wd_raw.at[j], s_wd.at[j])
-
-    def load_wg(j):
-        ref = w_gate if j % 2 == 0 else w_up
-        return pltpu.make_async_copy(
-            ref.at[pl.ds((j // 2) * CB, CB), :], wg_raw.at[j], s_wg.at[j]
-        )
-
-    small = [
-        pltpu.make_async_copy(ids, ids_v, s_small.at[0]),
-        pltpu.make_async_copy(route, route_v, s_small.at[1]),
-        pltpu.make_async_copy(layer_in, lin_v, s_small.at[2]),
-        pltpu.make_async_copy(gate_pre, gates.at[:, own_rows, :], s_small.at[3]),
-        pltpu.make_async_copy(up_pre, ups.at[:, own_rows, :], s_small.at[4]),
-        pltpu.make_async_copy(grad_out, go.at[n], s_small.at[5]),
-    ]
-    for copy in small:
-        copy.start()
-    for j in range(NODES):
-        load_wd(j).start()
-    for j in range(2 * NODES):
-        load_wg(j).start()
-
-    neighbours = jnp.minimum(s, 1) + jnp.minimum(SECTIONS - 1 - s, 1)
-    pl.semaphore_wait(
-        barrier,
-        NODES - 1 + DP - 1 + neighbours * NODES + lax.rem(s, 2) * (NODES - 1),
-    )
-
-    def send_go(q, half):
-        columns = pl.ds(half * HALF, HALF)
-        return remote(
-            grad_out.at[:, columns], go.at[n, :, columns], ss_go.at[q], rs_go.at[n, half],
-            section=SECTIONS - 1, node=near(n, OFFSETS[q]),
-        )
-
-    def send_gate(k):
-        return remote(
-            gate_pre, gates.at[:, own_rows, :], ss_gate.at[k], rs_gate.at[r], dp=peer(k)
-        )
-
-    def send_up(k):
-        return remote(
-            up_pre, ups.at[:, own_rows, :], ss_up.at[k], rs_up.at[r], dp=peer(k)
-        )
-
-    def send_lx(k):
-        return remote(
-            lsc.at[peer(k)], lx.at[r], ss_lx.at[k], rs_lx.at[r], dp=peer(k)
-        )
-
-    def send_lg(q):
-        return remote(lx, lg.at[n], ss_lg.at[q], rs_lg.at[n], node=near(n, OFFSETS[q]))
-
-    @pl.when(s == SECTIONS - 1)
-    def _():
-        for q in range(NODES - 1):
-            send_go(q, 0).start()
-
-    @pl.when(s == 1)
-    def _():
-        for q in range(NODES - 1):
-            send_go(q, 1).start()
 
     for copy in small:
         copy.wait()
@@ -175,15 +149,58 @@
         across = jnp.sum(
             jnp.where(ids_v[m] == 0, route_v[m], jnp.float32(0.0)), axis=0, keepdims=True
         )
+        crow[r, 0:1, m * ROWS : (m + 1) * ROWS] = across
         coef_v[m * ROWS : (m + 1) * ROWS, :] = jnp.sum(
             jnp.where(diagonal, across, jnp.float32(0.0)), axis=1, keepdims=True
         )
 
+    for i in range(NODES):
+        turn(i)
+
+    neighbours = jnp.minimum(s, 1) + jnp.minimum(SECTIONS - 1 - s, 1)
+    pl.semaphore_wait(
+        barrier,
+        NODES - 1 + DP - 1 + neighbours * NODES + lax.rem(s, 2) * (NODES - 1),
+    )
+
+    def send_go(q, half):
+        return remote(
+            go.at[n, half], go.at[n, half], ss_go.at[q], rs_go.at[n, half],
+            section=SECTIONS - 1, node=near(n, OFFSETS[q]),
+        )
+
+    def send_gate(k):
+        return remote(gates.at[r], gates.at[r], ss_gate.at[k], rs_gate.at[r], dp=peer(k))
+
+    def send_up(k):
+        return remote(ups.at[r], ups.at[r], ss_up.at[k], rs_up.at[r], dp=peer(k))
+
+    def send_lx(k):
+        return remote(
+            lsc.at[peer(k)], lx.at[r], ss_lx.at[k], rs_lx.at[r], dp=peer(k)
+        )
+
+    def send_cr(k):
+        return remote(crow.at[r], crow.at[r], ss_cr.at[k], rs_cr.at[r], dp=peer(k))
+
+    def send_lg(q):
+        return remote(lx, lg.at[n], ss_lg.at[q], rs_lg.at[n], node=near(n, OFFSETS[q]))
+
+    @pl.when(s == SECTIONS - 1)
+    def _():
+        for q in range(NODES - 1):
+            send_go(q, 0).start()
+
+    @pl.when(s == 1)
+    def _():
+        for q in range(NODES - 1):
+            send_go(q, 1).start()
+
     for m in range(MICRO):
-        gate = gates[m, own_rows, :].astype(F32)
+        gate = gates[r, m].astype(F32)
         active = jax.nn.sigmoid(gate) * coef_v[m * ROWS : (m + 1) * ROWS, :]
         factors[m, :, :HID] = (
-            ups[m, own_rows, :].astype(F32) * active * (1.0 + gate * (1.0 - jax.nn.sigmoid(gate)))
+            ups[r, m].astype(F32) * active * (1.0 + gate * (1.0 - jax.nn.sigmoid(gate)))
         )
         factors[m, :, HID:] = gate * active
 
@@ -199,23 +216,47 @@
             lsc[j] = (lin_v[:, j * DB : (j + 1) * DB].astype(F32) * scale).astype(BF16)
         lx[r] = lsc[r]
         for k in range(1, DP):
+            send_cr(k).start()
             send_lx(k).start()
         for k in range(1, DP):
             send_gate(k).start()
         for k in range(1, DP):
             send_up(k).start()
 
+    def take_gates():
+        for k in range(1, DP):
+            j = peer(k)
+            remote(gates.at[r], gates.at[j], ss_gate.at[k], rs_gate.at[j], dp=j).wait_recv()
+
+    def prepare_hidden():
+        for k in range(1, DP):
+            j = peer(k)
+            remote(ups.at[r], ups.at[j], ss_up.at[k], rs_up.at[j], dp=j).wait_recv()
+            remote(crow.at[r], crow.at[j], ss_cr.at[k], rs_cr.at[j], dp=j).wait_recv()
+        for m in range(MICRO):
+            for c in range(2):
+                pair = slice(2 * c, 2 * c + 2)
+                g = gates[pair, m].reshape(2 * ROWS, HID).astype(F32)
+                u = ups[pair, m].reshape(2 * ROWS, HID).astype(F32)
+                hidden = (g * jax.nn.sigmoid(g) * u).astype(BF16)
+                across = jnp.concatenate(
+                    [crow[2 * c + i, 0:1, m * ROWS : (m + 1) * ROWS] for i in range(2)], axis=1
+                )
+                hid_t[:, m * ALL + c * 128 : m * ALL + (c + 1) * 128] = (
+                    hidden.T.astype(F32) * across
+                ).astype(BF16)
+
+    def keep_lin():
+        return pltpu.make_async_copy(lin_t, lin_out, s_out.at[0])
+
     def gather_inputs():
         for k in range(1, DP):
             remote(lsc.at[0], lx.at[peer(k)], ss_lx.at[k], rs_lx.at[peer(k)], dp=peer(k)).wait_recv()
+        lg[n] = lx[...]
         for q in range(NODES - 1):
             send_lg(q).start()
-        lg[n] = lx[...]
-
-    def keep_lin():
-        return pltpu.make_async_copy(lin_t, lin_out, s_out.at[0])
-
-    def prepare():
+
+    def prepare_inputs():
         for offset in OFFSETS:
             j = near(n, offset)
             remote(lx, lg.at[j], ss_lg.at[0], rs_lg.at[j], node=j).wait_recv()
@@ -230,35 +271,23 @@
             )
             lin_t[:, m * ALL : (m + 1) * ALL] = rows.astype(BF16).T
         keep_lin().start()
-        for k in range(1, DP):
-            j = peer(k)
-            rows = pl.ds(pl.multiple_of(j * ROWS, ROWS), ROWS)
-            remote(gate_pre, gates.at[:, rows, :], ss_gate.at[k], rs_gate.at[j], dp=j).wait_recv()
-            remote(up_pre, ups.at[:, rows, :], ss_up.at[k], rs_up.at[j], dp=j).wait_recv()
-        for m in range(MICRO):
-            for c in range(2):
-                rows = pl.ds(c * 128, 128)
-                g = gates[m, rows, :].astype(F32)
-                hidden = (g * jax.nn.sigmoid(g) * ups[m, rows, :].astype(F32)).astype(BF16)
-                hid_t[:, m * ALL + c * 128 : m * ALL + (c + 1) * 128] = hidden.T
 
     @pl.when(s < 2)
     def _():
         exchange()
 
-    for j in range(NODES):
-        load_wd(j).wait()
-        wdt[j] = wd_raw[j].T
-    for j in range(NODES):
-        load_wg(2 * j).wait()
-        load_wg(2 * j + 1).wait()
-        wgut[j, :HID, :] = wg_raw[2 * j].T
-        wgut[j, HID:, :] = wg_raw[2 * j + 1].T
+    for i in range(NODES, PIECES):
+        turn(i)
 
     @pl.when(s < 2)
     def _():
         gather_inputs()
-        prepare()
+        take_gates()
+
+    @pl.when(s == 0)
+    def _():
+        prepare_hidden()
+        prepare_inputs()
 
     def send_ga(m, q):
         return remote(
@@ -269,32 +298,32 @@
         return remote(dyg.at[m, j], dyg.at[m, j], ss_ga.at[m, 0], rs_ga.at[m, j], node=j)
 
     def finish_back(m, back):
-        backs[m, own_rows, :] = back.astype(BF16)
+        backs[m, r] = back.astype(BF16)
         dgu[m, :, :HID] = (back * factors[m, :, :HID]).astype(BF16)
         dgu[m, :, HID:] = (back * factors[m, :, HID:]).astype(BF16)
 
-    def unpack(m, columns):
-        block = go[:, :, columns].astype(F32)
+    def unpack(m, half, columns):
+        block = go[:, half, :, columns].astype(F32)
         return block[:, m * OWN : (m + 1) * OWN, :].reshape(ROWS, CB).astype(BF16)
 
     @pl.when(s == SECTIONS - 1)
     def _():
         for half in range(2):
-            columns = pl.ds(half * HALF, HALF)
             for offset in OFFSETS:
                 j = near(n, offset)
                 remote(
-                    grad_out.at[:, columns], go.at[j, :, columns], ss_go.at[0], rs_go.at[j, half],
+                    go.at[n, half], go.at[j, half], ss_go.at[0], rs_go.at[j, half],
                     section=SECTIONS - 1, node=j,
                 ).wait_recv()
         back = jnp.zeros((MICRO * ROWS, HID), F32)
         for j in range(NODES):
-            block = go[:, :, j * CB : (j + 1) * CB].reshape(MICRO * ROWS, CB)
+            start = (j % 4) * CB
+            block = go[:, j // 4, :, start : start + CB].reshape(MICRO * ROWS, CB)
             back = back + dot(block, wdt[j])
         back = back.reshape(NODES, MICRO * OWN, HID)
         for m in range(MICRO):
             finish_back(m, back[:, m * OWN : (m + 1) * OWN, :].reshape(ROWS, HID))
-            dyg[m, n] = unpack(m, pl.ds(pl.multiple_of(n * CB, CB), CB))
+            dyg[m, n] = unpack(m, lax.div(n, 4), pl.ds(pl.multiple_of(lax.rem(n, 4) * CB, CB), CB))
 
     @pl.when(s < SECTIONS - 1)
     def _():
@@ -317,15 +346,12 @@
         )
 
     def send_b(m, k):
-        return remote(
-            backs.at[m, own_rows, :], backs.at[m, own_rows, :],
-            ss_b.at[m, k], rs_b.at[m, r], dp=peer(k),
-        )
+        return remote(backs.at[m, r], backs.at[m, r], ss_b.at[m, k], rs_b.at[m, r], dp=peer(k))
 
     def send_dy(m, k):
         return remote(
-            dys_send.at[m, k - 1], dys.at[m, :, own_rows, :],
-            ss_dy.at[m, k], rs_dy.at[m, r], dp=peer(k),
+            dyg.at[m, pl.ds(2 * peer(k), 2)], dys.at[m, r], ss_dy.at[m, k], rs_dy.at[m, r],
+            dp=peer(k),
         )
 
     def send_f(m, q, step):
@@ -350,16 +376,13 @@
         put(fr.at[m, n, half], n)
 
     def exchange_dy(m):
-        scale = coef_v[m * ROWS : (m + 1) * ROWS, :]
-        for k in range(DP):
-            for h in range(2):
-                value = (dyg[m, 2 * peer(k) + h].astype(F32) * scale).astype(BF16)
-                if k == 0:
-                    dys[m, h, own_rows, :] = value
-                else:
-                    dys_send[m, k - 1, h] = value
         for k in range(1, DP):
             send_dy(m, k).start()
+        dys[m, r] = dyg[m, pl.ds(2 * r, 2)]
+
+    def exchange_back(m):
+        for k in range(1, DP):
+            send_b(m, k).start()
 
     arrivals = (((0, 1), (0, 3)), ((0, 2), (1, 0)), ((1, 1), (1, 3), (1, 2)))
     order = OFFSETS + ((0, 0),)
@@ -371,6 +394,12 @@
             for group in arrivals:
                 for offset in group:
                     recv_ga(m, near(n, offset)).wait_recv()
+                if group is arrivals[-1]:
+
+                    @pl.when(s == 0)
+                    def _():
+                        exchange_dy(m)
+
                 for offset in group:
                     j = near(n, offset)
                     back = back + dot(dyg[m, j], wdt[j])
@@ -378,9 +407,7 @@
 
         @pl.when(s == 0)
         def _():
-            for k in range(1, DP):
-                send_b(m, k).start()
-            exchange_dy(m)
+            exchange_back(m)
 
         for g in range(NODES // 2):
             for offset in order[2 * g : 2 * g + 2]:
@@ -402,18 +429,20 @@
                 def _():
                     send_tokens(m, g // 2)
 
+        @pl.when(jnp.logical_and(s > 0, s < SECTIONS - 1))
+        def _():
+            exchange_back(m)
+            exchange_dy(m)
+
     @pl.when(s == SECTIONS - 1)
     def _():
         for m in range(MICRO):
             for j in range(NODES):
-                dyg[m, j] = unpack(m, slice(j * CB, (j + 1) * CB))
-
-    @pl.when(s > 0)
-    def _():
-        for m in range(MICRO):
-            for k in range(1, DP):
-                send_b(m, k).start()
-        for m in range(MICRO):
+                start = (j % 4) * CB
+                dyg[m, j] = unpack(m, j // 4, slice(start, start + CB))
+
+        for m in range(MICRO):
+            exchange_back(m)
             exchange_dy(m)
 
     def send_ret():
@@ -434,8 +463,30 @@
     @pl.when(s >= 2)
     def _():
         exchange()
+
+    @pl.when(s == 2)
+    def _():
         gather_inputs()
-        prepare()
+
+    @pl.when(s >= 2)
+    def _():
+        take_gates()
+
+    @pl.when(s > 0)
+    def _():
+        prepare_hidden()
+
+    def take_ret():
+        remote(ret, gi, ss_ret.at[0], rs_ret.at[0], section=below).wait_recv()
+
+    @pl.when(s == SECTIONS - 1)
+    def _():
+        take_ret()
+        gather_inputs()
+
+    @pl.when(s > 0)
+    def _():
+        prepare_inputs()
 
     def keep_d(which, m):
         staged, array = ((dga, dg_out), (dua, du_out))[which]
@@ -448,17 +499,14 @@
     def spread(m):
         for k in range(1, DP):
             j = peer(k)
-            rows = pl.ds(pl.multiple_of(j * ROWS, ROWS), ROWS)
-            remote(
-                backs.at[m, own_rows, :], backs.at[m, rows, :], ss_b.at[m, k], rs_b.at[m, j], dp=j
-            ).wait_recv()
+            remote(backs.at[m, r], backs.at[m, j], ss_b.at[m, k], rs_b.at[m, j], dp=j).wait_recv()
         for k in range(DP):
             rows = slice(k * ROWS, (k + 1) * ROWS)
-            back = backs[m, rows, :].astype(F32)
-            gate = gates[m, rows, :].astype(F32)
+            back = backs[m, k].astype(F32)
+            gate = gates[k, m].astype(F32)
             sigma = jax.nn.sigmoid(gate)
             dga[m, rows, :] = (
-                back * ups[m, rows, :].astype(F32) * sigma * (1.0 + gate * (1.0 - sigma))
+                back * ups[k, m].astype(F32) * sigma * (1.0 + gate * (1.0 - sigma))
             ).astype(BF16)
             dua[m, rows, :] = (back * gate * sigma).astype(BF16)
         keep_d(0, m).start()
@@ -468,17 +516,16 @@
     for m in range(MICRO):
         for k in range(1, DP):
             j = peer(k)
-            rows = pl.ds(pl.multiple_of(j * ROWS, ROWS), ROWS)
             remote(
-                dys_send.at[m, 0], dys.at[m, :, rows, :], ss_dy.at[m, k], rs_dy.at[m, j], dp=j
+                dyg.at[m, pl.ds(0, 2)], dys.at[m, j], ss_dy.at[m, k], rs_dy.at[m, j], dp=j
             ).wait_recv()
     for i in range(HID // 256):
         rows = slice(i * 256, (i + 1) * 256)
         for h in range(2):
-            value = dot(hid_t[rows, :ALL], dys[0, h]) + dot(hid_t[rows, ALL:], dys[1, h])
+            value = dot(hid_t[rows, :ALL], dys[0, :, h].reshape(ALL, CB))
+            value = value + dot(hid_t[rows, ALL:], dys[1, :, h].reshape(ALL, CB))
             gd[rows, h * CB : (h + 1) * CB] = value.astype(BF16)
         keep_down(i).start()
-    spread(1)
 
     @pl.when(s == 0)
     def _():
@@ -503,12 +550,13 @@
                     [total[c * OWN : (c + 1) * OWN] for total in totals], axis=0
                 ).astype(BF16)
 
-    @pl.when(s > 0)
-    def _():
-        remote(ret, gi, ss_ret.at[0], rs_ret.at[0], section=below).wait_recv()
-
-    last = pltpu.make_async_copy(gi, grad_in, s_small.at[6])
+    @pl.when(jnp.logical_and(s > 0, s < SECTIONS - 1))
+    def _():
+        take_ret()
+
+    last = pltpu.make_async_copy(gi, grad_in, s_small.at[7])
     last.start()
+    spread(1)
 
     @pl.when(s == SECTIONS - 1)
     def _():
@@ -524,6 +572,7 @@
         send_gate(k).wait_send()
         send_up(k).wait_send()
         send_lx(k).wait_send()
+        send_cr(k).wait_send()
     for q in range(NODES - 1):
         send_lg(q).wait_send()
     for m in range(MICRO):
@@ -604,7 +653,7 @@
     dma = pltpu.SemaphoreType.DMA
     vmem = pltpu.VMEM
     scratch = [
-        vmem((NODES, HID, CB), BF16),
+        vmem((NODES, HID // NODES, WIDTH), BF16),
         vmem((2 * NODES, CB, HID), BF16),
         vmem((NODES, CB, HID), BF16),
         vmem((NODES, 2 * HID, CB), BF16),
@@ -613,16 +662,16 @@
         vmem((both, WIDTH), BF16),
         vmem((MICRO * ROWS, 1), F32),
         vmem((MICRO, ROWS, 2 * HID), F32),
-        vmem((NODES, both, WIDTH), BF16),
+        vmem((NODES, 2, both, HALF), BF16),
         vmem((MICRO, NODES, ROWS, CB), BF16),
         vmem((MICRO, NODES, ROWS, CB), BF16),
         vmem((MICRO, NODES, ROWS, CB), BF16),
         vmem((MICRO, ROWS, 2 * HID), BF16),
-        vmem((MICRO, ALL, HID), BF16),
-        vmem((MICRO, ALL, HID), BF16),
-        vmem((MICRO, ALL, HID), BF16),
-        vmem((MICRO, 2, ALL, CB), BF16),
-        vmem((MICRO, DP - 1, 2, ROWS, CB), BF16),
+        vmem((DP, MICRO, ROWS, HID), BF16),
+        vmem((DP, MICRO, ROWS, HID), BF16),
+        vmem((MICRO, DP, ROWS, HID), BF16),
+        vmem((MICRO, DP, 2, ROWS, CB), BF16),
+        vmem((DP, 8, MICRO * ROWS), F32),
         vmem((DP, both, DB), BF16),
         vmem((DP, both, DB), BF16),
         vmem((NODES, DP, both, DB), BF16),
@@ -636,7 +685,7 @@
         vmem((NODES, NODES, OWN, CB), F32),
         vmem((MICRO, NODES - 1, 2, 16, 2 * CB), BF16),
         vmem((MICRO, NODES, 2, 16, 2 * CB), BF16),
-        dma((7,)),
+        dma((8,)),
         dma((NODES,)),
         dma((2 * NODES,)),
         dma((9,)),
@@ -654,6 +703,8 @@
         dma((DP,)),
         dma((NODES,)),
         dma((NODES,)),
+        dma((DP,)),
+        dma((DP,)),
         dma((MICRO, DP)),
         dma((MICRO, DP)),
         dma((MICRO, DP)),

time: 86.8 us -> 79.2 us (0.912)
  Pallas kernels: 85.9 us -> 77.6 us
    pallas_call x1, Pallas kernels: 81.5 us -> 73.2 us  [shards(): pl.pallas_call(body, out_shape=(jax.ShapeDtypeStruct((both, WIDTH), BF16)...]
where the time goes in v3:
time: 79.2 us; the launch traced here: 78.4 us
  Pallas kernels  77.6 us (98%)
  between operations  0.8 us (1%)
    pallas_call x1, Pallas kernels, shards(): pl.pallas_call(body, out_shape=(jax.ShapeDtypeStruct((both, WIDTH), BF16)...  73.2 us
    pallas_call x1, Pallas kernels, shards(): pl.pallas_call(finish, out_shape=(jax.ShapeDtypeStruct((both, WIDTH), BF1...  4.42 us

profile of v3, /device:TPU:0, one launch (start us, length us, event | category | flops | bytes accessed | tf_op | source)
XLA Modules:
  0.0 78.4 jit_solution(6146526462915667367)
XLA Ops:
  0.6 73.2 %relay.1 = (bf16[16,3072]{1,0:T(8,128)(2,1)}, bf16[768,512]{1,0:T(8,128)(2,1)}, bf16[2,256,1024]{2,1,0:T(8,128)(2,1)}, bf16[2,256,1024]{2,1,0:T(8,128)(2,1)}, bf16[1024,768]{1,0:T(8,128)(2,1)}) custom-call(bf16[16,3072]{1,0:T(8,128)(2,1)} %bitcast.22, bf16[16,3072]{1,0:T(8,128)(2,1)} %bitcast.23, bf16[2,64,1024]{2,1,0:T(8,128)(2,1)} %bitcast.20, ...), custom_call_target="tpu_custom_call" | custom-call | flops 5000000000 | bytes 24000000 | tf_op jit(solution)/shard_map/relay/pallas_call | solution.py:718
  73.9 4.4 %finish.1 = (bf16[16,3072]{1,0:T(8,128)(2,1)}, bf16[768,1024]{1,0:T(8,128)(2,1)}, bf16[768,1024]{1,0:T(8,128)(2,1)}, bf16[1024,768]{1,0:T(8,128)(2,1)}) custom-call(bf16[16,3072]{1,0:T(8,128)(2,1)} %get-tuple-element.13.grad_in, bf16[768,512]{1,0:T(8,128)(2,1)} %get-tuple-element.14.lin, bf16[2,256,1024]{2,1,0:T(8,128)(2,1)} %get-tuple-element.15.dg, ...), custom_call_target="tpu_custom_call" | custom-call | flops 1600000000 | bytes 10000000 | tf_op jit(solution)/shard_map/finish/pallas_call | solution.py:746

commit v4 on v3

--- a/solution.py
+++ b/solution.py
@@ -20,6 +20,7 @@
 CB = WIDTH // NODES
 DB = WIDTH // DP
 HALF = WIDTH // 2
+RING = 12
 WINDOW = 10
 PIECES = 3 * NODES
 OFFSETS = ((1, 2), (1, 1), (1, 3), (1, 0), (0, 2), (0, 1), (0, 3))
@@ -47,14 +48,14 @@
 
 def body(
     grad_out, layer_in, gate_pre, up_pre, ids, route, w_gate, w_up, w_down,
-    grad_in, lin_out, dg_out, du_out, gd_out,
+    grad_in, lin_t, dga, dua, gd,
     wd_raw, wg_raw, wdt, wgut,
     ids_v, route_v, lin_v, coef_v, factors,
     go, dyg, prt, snd, dgu,
     gates, ups, backs, dys, crow,
-    lsc, lx, lg, lin_t, hid_t, dga, dua, gd,
+    lsc, lx, lg, hid_t,
     ret, gi, fp, fs, fr,
-    s_small, s_wd, s_wg, s_out,
+    s_small, s_wd, s_wg,
     ss_go, rs_go, ss_sc, rs_sc, ss_ga, rs_ga,
     ss_gate, rs_gate, ss_up, rs_up, ss_lx, rs_lx, ss_lg, rs_lg,
     ss_cr, rs_cr, ss_b, rs_b, ss_dy, rs_dy, ss_ret, rs_ret, ss_f, rs_f,
@@ -76,7 +77,7 @@
         j = i - NODES
         ref = w_gate if j % 2 == 0 else w_up
         return pltpu.make_async_copy(
-            ref.at[pl.ds((j // 2) * CB, CB), :], wg_raw.at[j], s_wg.at[j]
+            ref.at[pl.ds((j // 2) * CB, CB), :], wg_raw.at[j % RING], s_wg.at[j]
         )
 
     def turn(i):
@@ -90,7 +91,7 @@
         else:
             j = i - NODES
             start = (j % 2) * HID
-            wgut[j // 2, start : start + HID, :] = wg_raw[j].T
+            wgut[j // 2, start : start + HID, :] = wg_raw[j % RING].T
 
     small = [
         pltpu.make_async_copy(ids, ids_v, s_small.at[0]),
@@ -246,9 +247,6 @@
                     hidden.T.astype(F32) * across
                 ).astype(BF16)
 
-    def keep_lin():
-        return pltpu.make_async_copy(lin_t, lin_out, s_out.at[0])
-
     def gather_inputs():
         for k in range(1, DP):
             remote(lsc.at[0], lx.at[peer(k)], ss_lx.at[k], rs_lx.at[peer(k)], dp=peer(k)).wait_recv()
@@ -270,7 +268,6 @@
                 axis=0,
             )
             lin_t[:, m * ALL : (m + 1) * ALL] = rows.astype(BF16).T
-        keep_lin().start()
 
     @pl.when(s < 2)
     def _():
@@ -488,14 +485,6 @@
     def _():
         prepare_inputs()
 
-    def keep_d(which, m):
-        staged, array = ((dga, dg_out), (dua, du_out))[which]
-        return pltpu.make_async_copy(staged.at[m], array.at[m], s_out.at[1 + 2 * which + m])
-
-    def keep_down(i):
-        rows = pl.ds(i * 256, 256)
-        return pltpu.make_async_copy(gd.at[rows, :], gd_out.at[rows, :], s_out.at[5 + i])
-
     def spread(m):
         for k in range(1, DP):
             j = peer(k)
@@ -509,8 +498,6 @@
                 back * ups[k, m].astype(F32) * sigma * (1.0 + gate * (1.0 - sigma))
             ).astype(BF16)
             dua[m, rows, :] = (back * gate * sigma).astype(BF16)
-        keep_d(0, m).start()
-        keep_d(1, m).start()
 
     spread(0)
     for m in range(MICRO):
@@ -525,7 +512,6 @@
             value = dot(hid_t[rows, :ALL], dys[0, :, h].reshape(ALL, CB))
             value = value + dot(hid_t[rows, ALL:], dys[1, :, h].reshape(ALL, CB))
             gd[rows, h * CB : (h + 1) * CB] = value.astype(BF16)
-        keep_down(i).start()
 
     @pl.when(s == 0)
     def _():
@@ -554,8 +540,7 @@
     def _():
         take_ret()
 
-    last = pltpu.make_async_copy(gi, grad_in, s_small.at[7])
-    last.start()
+    grad_in[...] = gi[...]
     spread(1)
 
     @pl.when(s == SECTIONS - 1)
@@ -600,49 +585,28 @@
                 for step in range(2):
                     send_f(m, q, step).wait_send()
 
-    keep_lin().wait()
-    for m in range(MICRO):
-        keep_d(0, m).wait()
-        keep_d(1, m).wait()
-    for i in range(HID // 256):
-        keep_down(i).wait()
-    last.wait()
-
 
 def finish(
     grad_in, lin, dg, du, down,
     o_in, o_gate, o_up, o_down,
-    in_v, lin_v, dg_v, du_v, down_v, gate_v, up_v, sems,
+    gate_v, up_v, sems,
 ):
-    loads = [
-        pltpu.make_async_copy(lin, lin_v, sems.at[0]),
-        pltpu.make_async_copy(dg, dg_v, sems.at[1]),
-        pltpu.make_async_copy(du, du_v, sems.at[2]),
-        pltpu.make_async_copy(down, down_v, sems.at[3]),
-        pltpu.make_async_copy(grad_in, in_v, sems.at[4]),
+    stores = [
+        pltpu.make_async_copy(down, o_down, sems.at[0]),
+        pltpu.make_async_copy(grad_in, o_in, sems.at[1]),
     ]
-    for copy in loads:
+    for copy in stores:
         copy.start()
-    stores = []
-    loads[0].wait()
-    for which, (d, staged, out) in enumerate(((dg_v, gate_v, o_gate), (du_v, up_v, o_up))):
-        loads[1 + which].wait()
+    for which, (d, staged, out) in enumerate(((dg, gate_v, o_gate), (du, up_v, o_up))):
         for i in range(DB // 256):
             rows = pl.ds(i * 256, 256)
-            value = dot(lin_v[rows, :ALL], d[0]) + dot(lin_v[rows, ALL:], d[1])
+            value = dot(lin[rows, :ALL], d[0]) + dot(lin[rows, ALL:], d[1])
             staged[rows, :] = value.astype(BF16)
             stores.append(
                 pltpu.make_async_copy(
-                    staged.at[rows, :], out.at[rows, :], sems.at[7 + 3 * which + i]
+                    staged.at[rows, :], out.at[rows, :], sems.at[2 + 3 * which + i]
                 )
             )
-            stores[-1].start()
-        if which == 0:
-            loads[3].wait()
-            loads[4].wait()
-            stores.append(pltpu.make_async_copy(down_v, o_down, sems.at[5]))
-            stores.append(pltpu.make_async_copy(in_v, o_in, sems.at[6]))
-            stores[-2].start()
             stores[-1].start()
     for copy in stores:
         copy.wait()
@@ -654,7 +618,7 @@
     vmem = pltpu.VMEM
     scratch = [
         vmem((NODES, HID // NODES, WIDTH), BF16),
-        vmem((2 * NODES, CB, HID), BF16),
+        vmem((RING, CB, HID), BF16),
         vmem((NODES, CB, HID), BF16),
         vmem((NODES, 2 * HID, CB), BF16),
         vmem((MICRO, 2, ROWS), jnp.int32),
@@ -675,11 +639,7 @@
         vmem((DP, both, DB), BF16),
         vmem((DP, both, DB), BF16),
         vmem((NODES, DP, both, DB), BF16),
-        vmem((DB, MICRO * ALL), BF16),
         vmem((HID, MICRO * ALL), BF16),
-        vmem((MICRO, ALL, HID), BF16),
-        vmem((MICRO, ALL, HID), BF16),
-        vmem((HID, DB), BF16),
         vmem((both, WIDTH), BF16),
         vmem((both, WIDTH), BF16),
         vmem((NODES, NODES, OWN, CB), F32),
@@ -688,7 +648,6 @@
         dma((8,)),
         dma((NODES,)),
         dma((2 * NODES,)),
-        dma((9,)),
         dma((NODES,)),
         dma((NODES, 2)),
         dma((MICRO, NODES)),
@@ -715,20 +674,21 @@
         dma((MICRO, NODES, 2)),
     ]
     anywhere = pl.BlockSpec(memory_space=pl.ANY)
+    inside = pl.BlockSpec(memory_space=pltpu.VMEM)
     left = pl.pallas_call(
         body,
         out_shape=(
-            jax.ShapeDtypeStruct((both, WIDTH), BF16),
-            jax.ShapeDtypeStruct((DB, MICRO * ALL), BF16),
-            jax.ShapeDtypeStruct((MICRO, ALL, HID), BF16),
-            jax.ShapeDtypeStruct((MICRO, ALL, HID), BF16),
-            jax.ShapeDtypeStruct((HID, DB), BF16),
+            vmem((both, WIDTH), BF16),
+            vmem((DB, MICRO * ALL), BF16),
+            vmem((MICRO, ALL, HID), BF16),
+            vmem((MICRO, ALL, HID), BF16),
+            vmem((HID, DB), BF16),
         ),
         in_specs=[anywhere] * 9,
-        out_specs=(anywhere,) * 5,
+        out_specs=(inside,) * 5,
         scratch_shapes=scratch,
         compiler_params=pltpu.CompilerParams(
-            collective_id=0, has_side_effects=True, vmem_limit_bytes=62 * 2**20
+            collective_id=0, has_side_effects=True, vmem_limit_bytes=53 * 2**20
         ),
         cost_estimate=pl.CostEstimate(flops=5 * 10**9, bytes_accessed=24 * 10**6, transcendentals=10**6),
         name="relay",
@@ -751,22 +711,17 @@
             jax.ShapeDtypeStruct((DB, HID), BF16),
             jax.ShapeDtypeStruct((HID, DB), BF16),
         ),
-        in_specs=[anywhere] * 5,
+        in_specs=[inside] * 5,
         out_specs=(anywhere,) * 4,
         scratch_shapes=[
-            vmem((both, WIDTH), BF16),
-            vmem((DB, MICRO * ALL), BF16),
-            vmem((MICRO, ALL, HID), BF16),
-            vmem((MICRO, ALL, HID), BF16),
-            vmem((HID, DB), BF16),
             vmem((DB, HID), BF16),
             vmem((DB, HID), BF16),
-            dma((13,)),
+            dma((8,)),
         ],
-        compiler_params=pltpu.CompilerParams(vmem_limit_bytes=62 * 2**20),
+        compiler_params=pltpu.CompilerParams(vmem_limit_bytes=30 * 2**20),
         cost_estimate=pl.CostEstimate(flops=16 * 10**8, bytes_accessed=10**7, transcendentals=0),
         name="finish",
-    )(*left)
+    )(*(pltpu.with_memory_space_constraint(x, pltpu.VMEM) for x in left))
     return grad_in.reshape(1, MICRO, OWN, WIDTH), g_gate[None], g_up[None], g_down[None]
 
 

time: 79.2 us -> 76.7 us (0.968)
  Pallas kernels: 77.6 us -> 75.1 us
    pallas_call x1, Pallas kernels: 4.42 us -> 2.67 us  [shards(): pl.pallas_call(finish, out_shape=(jax.ShapeDtypeStruct((both, WIDTH), BF1...]
where the time goes in v4:
time: 76.7 us; the launch traced here: 75.9 us
  Pallas kernels  75.1 us (98%)
  between operations  0.8 us (1%)
    pallas_call x1, Pallas kernels, shards(): pl.pallas_call(body, out_shape=(vmem((both, WIDTH), BF16), vmem((DB, MICR...  72.4 us
    pallas_call x1, Pallas kernels, shards(): pl.pallas_call(finish, out_shape=(jax.ShapeDtypeStruct((both, WIDTH), BF1...  2.67 us

profile of v4, /device:TPU:0, one launch (start us, length us, event | category | flops | bytes accessed | tf_op | source)
XLA Modules:
  0.0 75.9 jit_solution(6971766308056575457)
XLA Ops:
  0.6 72.4 %relay.1 = (bf16[16,3072]{1,0:T(8,128)(2,1)S(1)}, bf16[768,512]{1,0:T(8,128)(2,1)S(1)}, bf16[2,256,1024]{2,1,0:T(8,128)(2,1)S(1)}, bf16[2,256,1024]{2,1,0:T(8,128)(2,1)S(1)}, bf16[1024,768]{1,0:T(8,128)(2,1)S(1)}) custom-call(bf16[16,3072]{1,0:T(8,128)(2,1)} %bitcast.22, bf16[16,3072]{1,0:T(8,128)(2,1)} %bitcast.23, bf16[2,64,1024]{2,1,0:T(8,128)(2,1)} %bitcast.20, ...), custom_call_target="tpu_custom_call" | custom-call | flops 5000000000 | bytes 24000000 | tf_op jit(solution)/shard_map/relay/pallas_call | solution.py:678
  73.1 2.7 %finish.1 = (bf16[16,3072]{1,0:T(8,128)(2,1)}, bf16[768,1024]{1,0:T(8,128)(2,1)}, bf16[768,1024]{1,0:T(8,128)(2,1)}, bf16[1024,768]{1,0:T(8,128)(2,1)}) custom-call(bf16[16,3072]{1,0:T(8,128)(2,1)S(1)} %get-tuple-element.13.grad_in, bf16[768,512]{1,0:T(8,128)(2,1)S(1)} %get-tuple-element.14.lin, bf16[2,256,1024]{2,1,0:T(8,128)(2,1)S(1)} %get-tuple-element.15.dg, ...), custom_call_target="tpu_custom_call" | custom-call | flops 1600000000 | bytes 10000000 | tf_op jit(solution)/shard_map/finish/pallas_call | solution.py:706

commit v5 on v4

--- a/solution.py
+++ b/solution.py
@@ -58,7 +58,7 @@
     s_small, s_wd, s_wg,
     ss_go, rs_go, ss_sc, rs_sc, ss_ga, rs_ga,
     ss_gate, rs_gate, ss_up, rs_up, ss_lx, rs_lx, ss_lg, rs_lg,
-    ss_cr, rs_cr, ss_b, rs_b, ss_dy, rs_dy, ss_ret, rs_ret, ss_f, rs_f,
+    ss_fw, rs_fw, ss_cr, rs_cr, ss_b, rs_b, ss_dy, rs_dy, ss_ret, rs_ret, ss_f, rs_f,
 ):
     s = lax.axis_index("section")
     r = lax.axis_index("dp")
@@ -176,6 +176,14 @@
     def send_up(k):
         return remote(ups.at[r], ups.at[r], ss_up.at[k], rs_up.at[r], dp=peer(k))
 
+    def forward(which, half):
+        array = (gates, ups)[which]
+        block = array.at[peer((DP - 1, 1)[half]), half]
+        return remote(
+            block, block, ss_fw.at[2 * which + half], rs_fw.at[2 * which + half],
+            dp=peer((1, DP - 1)[half]),
+        )
+
     def send_lx(k):
         return remote(
             lsc.at[peer(k)], lx.at[r], ss_lx.at[k], rs_lx.at[r], dp=peer(k)
@@ -219,21 +227,32 @@
         for k in range(1, DP):
             send_cr(k).start()
             send_lx(k).start()
-        for k in range(1, DP):
+        for k in (1, DP - 1):
             send_gate(k).start()
-        for k in range(1, DP):
+        for k in (1, DP - 1):
             send_up(k).start()
 
     def take_gates():
-        for k in range(1, DP):
+        for k in (1, DP - 1):
             j = peer(k)
             remote(gates.at[r], gates.at[j], ss_gate.at[k], rs_gate.at[j], dp=j).wait_recv()
+        for half in range(2):
+            forward(0, half).start()
+        for k in (1, DP - 1):
+            j = peer(k)
+            remote(ups.at[r], ups.at[j], ss_up.at[k], rs_up.at[j], dp=j).wait_recv()
+        for half in range(2):
+            forward(1, half).start()
 
     def prepare_hidden():
         for k in range(1, DP):
             j = peer(k)
-            remote(ups.at[r], ups.at[j], ss_up.at[k], rs_up.at[j], dp=j).wait_recv()
             remote(crow.at[r], crow.at[j], ss_cr.at[k], rs_cr.at[j], dp=j).wait_recv()
+        for which, array in enumerate((gates, ups)):
+            for half in range(2):
+                place = array.at[peer(2), half]
+                i = 2 * which + half
+                remote(place, place, ss_fw.at[i], rs_fw.at[i], dp=peer(1)).wait_recv()
         for m in range(MICRO):
             for c in range(2):
                 pair = slice(2 * c, 2 * c + 2)
@@ -406,8 +425,8 @@
         def _():
             exchange_back(m)
 
-        for g in range(NODES // 2):
-            for offset in order[2 * g : 2 * g + 2]:
+        for g in range(2):
+            for offset in order[4 * g : 4 * g + 4]:
                 j = near(n, offset)
                 part = dot(dgu[m], wgut[j])
                 if offset == (0, 0):
@@ -417,14 +436,14 @@
 
             @pl.when(s > 0)
             def _():
-                for offset in order[2 * g : 2 * g + 2]:
+                for offset in order[4 * g : 4 * g + 4]:
                     send_sc(m, near(n, offset)).start()
 
-            if g % 2 == 1:
+            if True:
 
                 @pl.when(s == 0)
                 def _():
-                    send_tokens(m, g // 2)
+                    send_tokens(m, g)
 
         @pl.when(jnp.logical_and(s > 0, s < SECTIONS - 1))
         def _():
@@ -554,12 +573,16 @@
             send_go(q, 1).wait_send()
 
     for k in range(1, DP):
-        send_gate(k).wait_send()
-        send_up(k).wait_send()
+        if k != 2:
+            send_gate(k).wait_send()
+            send_up(k).wait_send()
         send_lx(k).wait_send()
         send_cr(k).wait_send()
     for q in range(NODES - 1):
         send_lg(q).wait_send()
+    for which in range(2):
+        for half in range(2):
+            forward(which, half).wait_send()
     for m in range(MICRO):
         for k in range(1, DP):
             send_b(m, k).wait_send()
@@ -662,6 +685,8 @@
         dma((DP,)),
         dma((NODES,)),
         dma((NODES,)),
+        dma((4,)),
+        dma((4,)),
         dma((DP,)),
         dma((DP,)),
         dma((MICRO, DP)),

time: 76.7 us -> 76.1 us (level)
  no operation moved by 1% of the time
where the time goes in v5:
time: 76.1 us; the launch traced here: 76 us
  Pallas kernels  75.2 us (99%)
  between operations  0.8 us (1%)
    pallas_call x1, Pallas kernels, shards(): pl.pallas_call(body, out_shape=(vmem((both, WIDTH), BF16), vmem((DB, MICR...  72.5 us
    pallas_call x1, Pallas kernels, shards(): pl.pallas_call(finish, out_shape=(jax.ShapeDtypeStruct((both, WIDTH), BF1...  2.67 us

profile of v5, /device:TPU:0, one launch (start us, length us, event | category | flops | bytes accessed | tf_op | source)
XLA Modules:
  0.0 76.0 jit_solution(11611852442308891577)
XLA Ops:
  0.6 72.5 %relay.1 = (bf16[16,3072]{1,0:T(8,128)(2,1)S(1)}, bf16[768,512]{1,0:T(8,128)(2,1)S(1)}, bf16[2,256,1024]{2,1,0:T(8,128)(2,1)S(1)}, bf16[2,256,1024]{2,1,0:T(8,128)(2,1)S(1)}, bf16[1024,768]{1,0:T(8,128)(2,1)S(1)}) custom-call(bf16[16,3072]{1,0:T(8,128)(2,1)} %bitcast.22, bf16[16,3072]{1,0:T(8,128)(2,1)} %bitcast.23, bf16[2,64,1024]{2,1,0:T(8,128)(2,1)} %bitcast.20, ...), custom_call_target="tpu_custom_call" | custom-call | flops 5000000000 | bytes 24000000 | tf_op jit(solution)/shard_map/relay/pallas_call | solution.py:703
  73.2 2.7 %finish.1 = (bf16[16,3072]{1,0:T(8,128)(2,1)}, bf16[768,1024]{1,0:T(8,128)(2,1)}, bf16[768,1024]{1,0:T(8,128)(2,1)}, bf16[1024,768]{1,0:T(8,128)(2,1)}) custom-call(bf16[16,3072]{1,0:T(8,128)(2,1)S(1)} %get-tuple-element.13.grad_in, bf16[768,512]{1,0:T(8,128)(2,1)S(1)} %get-tuple-element.14.lin, bf16[2,256,1024]{2,1,0:T(8,128)(2,1)S(1)} %get-tuple-element.15.dg, ...), custom_call_target="tpu_custom_call" | custom-call | flops 1600000000 | bytes 10000000 | tf_op jit(solution)/shard_map/finish/pallas_call | solution.py:731
